TPU v7x, 32 devices: a whole 2x2x4 slice. The times are simulated.
32 devices in a mesh: groups: 2 (over y), gx: 4 (over z), gy: 2 (over x), gz: 2 (over core).
Axes of the slice: x: 2, y: 2, z: 4, core: 2. Of those that a mesh axis runs over, the one named last changes fastest.
Arguments:
- node_feats: bfloat16 [4096, 128], P(('groups', 'gx', 'gy', 'gz')), parts along dimension 0, may hold values from -6 to 6
- species: int32 [4096], P(('groups', 'gx', 'gy', 'gz')), parts along dimension 0, may hold values from 0 to 7
- export_index: int32 [512], P(('groups', 'gx', 'gy', 'gz')), parts along dimension 0, may hold values from 0 to 127
- pair_first: int32 [32768], P(('groups', 'gx', 'gy', 'gz')), parts along dimension 0, may hold values from 0 to 127, as said below
- pair_second: int32 [32768], P(('groups', 'gx', 'gy', 'gz')), parts along dimension 0, may hold values from 0 to 559, as said below
- pair_live: int32 [32768], P(('groups', 'gx', 'gy', 'gz')), parts along dimension 0, may hold values 0 or 1
- displacement: float32 [3, 32768], P(None, ('groups', 'gx', 'gy', 'gz')), parts along dimension 1, may hold values from -2.8 to 2.8, as said below
- w_up: bfloat16 [128, 128], replicated, may hold values from -0.5 to 0.5
- radial_one: float32 [8, 64], replicated, may hold values from -2 to 2
- radial_two: float32 [64, 64], replicated, may hold values from -0.75 to 0.75
- radial_three: float32 [64, 384], replicated, may hold values from -0.75 to 0.75
- power_weight: float32 [3, 128], replicated, may hold values from 0.2 to 1
- w_mix: bfloat16 [128, 128], replicated, may hold values from -0.5 to 0.5
- read_table: float32 [8, 128], replicated, may hold values from -0.5 to 0.5
- base_energy: float32 [8], replicated, may hold values from -3 to -1
Outputs:
- atom_energy: float32 [4096], P(('groups', 'gx', 'gy', 'gz')), parts along dimension 0
- pair_forces: float32 [3, 4096], P(None, ('groups', 'gx', 'gy', 'gz')), parts along dimension 1
- feats_grad: bfloat16 [4096, 128], P(('groups', 'gx', 'gy', 'gz')), parts along dimension 0
There are 2 independent parts, one for each index of `groups`. A program takes and returns all parts, laid end to end along the dimension named above; an argument that names none is the same for every part. Nothing has to cross between parts.
Inputs may be any that keep to these rules, and one draw needn't show every extreme that they name: `export_index`: entries may repeat. `pair_first`: A local row of the pair's domain. `pair_second`: A domain's pair slots h < 592 and its slots 1024 - 27 * 16 + 13 * 16 + r (r < 16) name a local row below 128 other than the pair's first atom; its slot 592 + g * 16 + r with g != 13 names 128 + g * 16 + e for some e below 16, a ghost slot of block g = 9 a + 3 b + c. `displacement`: each component's magnitude is at least 0.8.
All inputs are finite; a program needn't handle non-finite values. No bound on the sum of `pair_live` on one device may be relied on, other than what follows from the above.
Results may differ from a plain program's by a relative error of at most 0.0061.
Values may be sent and summed in bfloat16 or wider, within the bound.
A program may use at most 64 MiB of HBM per device.

v0:
```python
import math

import jax
import jax.numpy as jnp
from jax import lax
from jax.sharding import PartitionSpec as P

PRECISE = lax.Precision.HIGHEST
CUTOFF = 5.0
ROOT_THREE = math.sqrt(3.0)
ROOT_FIVE = math.sqrt(5.0)
ROOT_FIFTEEN = math.sqrt(15.0)
PARITY_SIGNS = (1.0, -1.0, -1.0, -1.0, 1.0, 1.0, 1.0, 1.0, 1.0)


def padded(value, sides, width):
    for axis, dim in sides:
        peers, length = (lax.axis_size(axis), value.shape[dim])
        up = [(i, (i + 1) % peers) for i in range(peers)]
        down = [(j, i) for i, j in up]
        last = lax.slice_in_dim(value, length - width, length, axis=dim)
        first = lax.slice_in_dim(value, 0, width, axis=dim)
        before = lax.ppermute(last, axis, up)
        after = lax.ppermute(first, axis, down)
        value = jnp.concatenate([before, value, after], axis=dim)
    return value


def harmonics(direction):
    along_x = direction[:, 0]
    along_y = direction[:, 1]
    along_z = direction[:, 2]
    constant = jnp.ones_like(along_x)
    return jnp.stack(
        [
            constant,
            ROOT_THREE * along_x,
            ROOT_THREE * along_y,
            ROOT_THREE * along_z,
            ROOT_FIFTEEN * along_x * along_z,
            ROOT_FIFTEEN * along_x * along_y,
            ROOT_FIVE * (along_y * along_y - 0.5 * (along_x * along_x + along_z * along_z)),
            ROOT_FIFTEEN * along_y * along_z,
            0.5 * ROOT_FIFTEEN * (along_z * along_z - along_x * along_x),
        ],
        axis=1,
    )


def geometry(vectors, radial_one, radial_two, radial_three):
    distance = jnp.sqrt(jnp.sum(vectors * vectors, axis=1))
    direction = vectors / distance[:, None]
    scaled = distance / CUTOFF
    orders = jnp.arange(1, radial_one.shape[0] + 1, dtype=jnp.float32)
    bessel = (
        math.sqrt(2.0 / CUTOFF)
        * jnp.sin(math.pi * orders[None, :] * scaled[:, None])
        / distance[:, None]
    )
    envelope = 1.0 - 28.0 * scaled**6 + 48.0 * scaled**7 - 21.0 * scaled**8
    basis_rows = bessel * envelope[:, None]
    hidden_one = jax.nn.silu(jnp.dot(basis_rows, radial_one, precision=PRECISE))
    hidden_two = jax.nn.silu(jnp.dot(hidden_one, radial_two, precision=PRECISE))
    radial = jnp.dot(hidden_two, radial_three, precision=PRECISE)
    return (harmonics(direction), radial.reshape(vectors.shape[0], 3, -1))


def spread_degrees(values):
    return jnp.concatenate(
        [
            values[:, 0:1],
            jnp.repeat(values[:, 1:2], 3, axis=1),
            jnp.repeat(values[:, 2:3], 5, axis=1),
        ],
        axis=1,
    )


def gather_degrees(values):
    return jnp.stack(
        [values[:, 0], jnp.sum(values[:, 1:4], axis=1), jnp.sum(values[:, 4:9], axis=1)], axis=1
    )


def pair_messages(vectors, first_up, second_up, weight, radial_one, radial_two, radial_three):
    harmonic, radial = geometry(vectors, radial_one, radial_two, radial_three)
    parity = jnp.asarray(PARITY_SIGNS, dtype=jnp.float32)
    spread = spread_degrees(radial) * weight[:, None, None]
    toward_first = spread * harmonic[:, :, None] * second_up[:, None, :]
    toward_second = spread * (harmonic * parity)[:, :, None] * first_up[:, None, :]
    return (toward_first, toward_second)


def pair_gradients(
    vectors,
    first_up,
    second_up,
    first_grad,
    second_grad,
    weight,
    radial_one,
    radial_two,
    radial_three,
):

    def shape_terms(moved_vectors):
        return geometry(moved_vectors, radial_one, radial_two, radial_three)

    (harmonic, radial), pullback = jax.vjp(shape_terms, vectors)
    parity = jnp.asarray(PARITY_SIGNS, dtype=jnp.float32)
    spread = spread_degrees(radial)
    lean_first = first_grad * harmonic[:, :, None]
    lean_second = second_grad * (harmonic * parity)[:, :, None]
    grad_spread = weight[:, None, None] * (
        lean_first * second_up[:, None, :] + lean_second * first_up[:, None, :]
    )
    up_second = weight[:, None] * jnp.sum(lean_first * spread, axis=1)
    up_first = weight[:, None] * jnp.sum(lean_second * spread, axis=1)
    grad_harmonic = weight[:, None] * (
        jnp.sum(first_grad * spread * second_up[:, None, :], axis=2)
        + parity * jnp.sum(second_grad * spread * first_up[:, None, :], axis=2)
    )
    (grad_vectors,) = pullback((grad_harmonic, gather_degrees(grad_spread)))
    return (up_first, up_second, grad_vectors)


def node_terms(amps, species, power_weight, w_mix, read_table, base_energy):
    squares = amps * amps
    product = (
        amps[:, 0]
        + power_weight[0] * squares[:, 0]
        + power_weight[1] * jnp.sum(squares[:, 1:4], axis=1)
        + power_weight[2] * jnp.sum(squares[:, 4:9], axis=1)
    ).astype(jnp.bfloat16)
    mixed_rows = jnp.dot(product, w_mix, preferred_element_type=jnp.float32)
    picker = (species[:, None] == jnp.arange(read_table.shape[0], dtype=jnp.int32)[None, :]).astype(
        jnp.float32
    )
    read_rows = jnp.dot(picker, read_table, precision=PRECISE)
    offsets = jnp.dot(picker, base_energy, precision=PRECISE)
    sigmoid = jax.nn.sigmoid(mixed_rows)
    energy = jnp.sum(mixed_rows * sigmoid * read_rows, axis=1) + offsets
    grad_mixed = (read_rows * sigmoid * (1.0 + mixed_rows * (1.0 - sigmoid))).astype(jnp.bfloat16)
    grad_product = jnp.dot(grad_mixed, w_mix.T, preferred_element_type=jnp.float32)
    first_hot = (jnp.arange(9, dtype=jnp.int32) == 0).astype(jnp.float32)
    power_spread = spread_degrees(power_weight[None])[0]
    grad_amps = (
        grad_product[:, None, :] * (first_hot[None, :, None] + 2.0 * power_spread[None] * amps)
    ).astype(jnp.bfloat16)
    return (energy, grad_amps)


def to_ghosts(rows, slot_count):
    packed = rows.reshape(1, 1, 1, slot_count, rows.shape[1])
    beside_all = padded(packed, (("gx", 0), ("gy", 1), ("gz", 2)), 1)
    return beside_all.reshape(27 * slot_count, rows.shape[1])


def on_device(
    node_feats,
    species,
    export_index,
    pair_first,
    pair_second,
    pair_live,
    displacement,
    w_up,
    radial_one,
    radial_two,
    radial_three,
    power_weight,
    w_mix,
    read_table,
    base_energy,
):
    atom_count, channels = node_feats.shape
    slot_count = export_index.shape[0]
    pair_count = pair_first.shape[0]
    up_own = jnp.dot(node_feats, w_up, preferred_element_type=jnp.float32).astype(jnp.bfloat16)
    ghost_feats = to_ghosts(node_feats[export_index], slot_count)
    ghost_up = jnp.dot(ghost_feats, w_up, preferred_element_type=jnp.float32).astype(jnp.bfloat16)
    node_up = jnp.concatenate([up_own, ghost_up], axis=0)
    node_count = node_up.shape[0]
    block_rows = min(512, pair_count)
    block_count = pair_count // block_rows
    weight_all = pair_live.astype(jnp.float32) / math.sqrt(2.0 * pair_count / atom_count)
    pair_vectors = displacement.T
    pair_blocks = (
        pair_first.reshape(block_count, block_rows),
        pair_second.reshape(block_count, block_rows),
        weight_all.reshape(block_count, block_rows),
        pair_vectors.reshape(block_count, block_rows, 3),
    )

    def gather_step(amp_table, blocks):
        first_rows, second_rows, weight, vectors = blocks
        toward_first, toward_second = pair_messages(
            vectors,
            node_up[first_rows].astype(jnp.float32),
            node_up[second_rows].astype(jnp.float32),
            weight,
            radial_one,
            radial_two,
            radial_three,
        )
        amp_table = amp_table.at[first_rows].add(toward_first).at[second_rows].add(toward_second)
        return (amp_table, None)

    amps_nodes, unused = lax.scan(
        gather_step, jnp.zeros((node_count, 9, channels), jnp.float32), pair_blocks
    )
    ghost_amps = amps_nodes[atom_count:].reshape(3, 3, 3, slot_count, 9 * channels)
    beside_all = padded(ghost_amps, (("gx", 0), ("gy", 1), ("gz", 2)), 1)
    returned = jnp.sum(beside_all[0::2, 0::2, 0::2], axis=(0, 1, 2))
    amps = amps_nodes[:atom_count].at[export_index].add(returned.reshape(slot_count, 9, channels))
    energy, grad_amps = node_terms(amps, species, power_weight, w_mix, read_table, base_energy)
    outgoing = grad_amps[export_index].reshape(1, 1, 1, slot_count, 9 * channels)
    ghost_grad = padded(outgoing, (("gx", 0), ("gy", 1), ("gz", 2)), 1)
    node_grad = jnp.concatenate(
        [grad_amps, ghost_grad.reshape(27 * slot_count, 9, channels)], axis=0
    )

    def grad_step(tables, blocks):
        up_table, force_table = tables
        first_rows, second_rows, weight, vectors = blocks
        up_first, up_second, grad_vectors = pair_gradients(
            vectors,
            node_up[first_rows].astype(jnp.float32),
            node_up[second_rows].astype(jnp.float32),
            node_grad[first_rows].astype(jnp.float32),
            node_grad[second_rows].astype(jnp.float32),
            weight,
            radial_one,
            radial_two,
            radial_three,
        )
        up_table = up_table.at[first_rows].add(up_first).at[second_rows].add(up_second)
        force_table = (
            force_table.at[first_rows].add(grad_vectors).at[second_rows].add(-grad_vectors)
        )
        return ((up_table, force_table), None)

    start = (
        jnp.zeros((node_count, channels), jnp.float32),
        jnp.zeros((node_count, 3), jnp.float32),
    )
    (up_nodes, force_nodes), unused = lax.scan(grad_step, start, pair_blocks)
    ghost_up_grad = up_nodes[atom_count:].reshape(3, 3, 3, slot_count, channels)
    ghost_force = jnp.transpose(
        force_nodes[atom_count:].reshape(3, 3, 3, slot_count, 3), (0, 1, 2, 4, 3)
    )
    around_up, around_force = (
        padded(ghost_up_grad, (("gx", 0), ("gy", 1), ("gz", 2)), 1),
        padded(ghost_force, (("gx", 0), ("gy", 1), ("gz", 2)), 1),
    )
    back_up = jnp.sum(around_up[0::2, 0::2, 0::2], axis=(0, 1, 2))
    back_force = jnp.sum(around_force[0::2, 0::2, 0::2], axis=(0, 1, 2))
    up_total = up_nodes[:atom_count].at[export_index].add(back_up)
    force_total = force_nodes[:atom_count].at[export_index].add(back_force.T)
    feats_grad = jnp.dot(
        up_total.astype(jnp.bfloat16), w_up.T, preferred_element_type=jnp.float32
    ).astype(jnp.bfloat16)
    return (energy, force_total.T, feats_grad)


def solution(mesh):
    in_specs = (
        P(("groups", "gx", "gy", "gz"), None),
        P(("groups", "gx", "gy", "gz")),
        P(("groups", "gx", "gy", "gz")),
        P(("groups", "gx", "gy", "gz")),
        P(("groups", "gx", "gy", "gz")),
        P(("groups", "gx", "gy", "gz")),
        P(None, ("groups", "gx", "gy", "gz")),
        P(),
        P(),
        P(),
        P(),
        P(),
        P(),
        P(),
        P(),
    )
    out_specs = (
        P(("groups", "gx", "gy", "gz")),
        P(None, ("groups", "gx", "gy", "gz")),
        P(("groups", "gx", "gy", "gz"), None),
    )
    return jax.shard_map(
        on_device, mesh=mesh, in_specs=in_specs, out_specs=out_specs, check_vma=False
    )
```

profile of v0, /device:TPU:0, one launch (start us, length us, event | category | flops | bytes accessed | tf_op | source)
XLA Modules:
  0.0 638.8 jit_solution(1544161306935728581)
XLA Ops:
  3.3 5.1 collective-permute-start.1
  9.7 4.1 collective-permute-done
  23.6 2.4 broadcast_in_dim.12
  26.0 306.1 %while.24 = (s32[]{:T(128)}, f32[560,9,128]{2,1,0:T(8,128)}, s32[2,512]{1,0:T(2,128)}, f32[2,512,3]{1,2,0:T(4,128)}, f32[8,64]{1,0:T(8,128)S(1)}, /*index=5*/f32...) while((s32[]{:T(128)}, f32[560,9,128]{2,1,0:T(8,128)}, ...), condition=%wide.region_4.5_spmd.clone, body=%wide.region_0.4_spmd.sunk.clone.sunk | while | flops 185053712 | bytes 30716340 | solution.py:209
  32.6 1.8 copy.180
  45.2 9.2 %fusion.207 = (f32[512,9,128]{2,1,0:T(8,128)}, f32[512,9,128]{2,1,0:T(8,128)}) fusion(f32[512,5,128]{2,1,0:T(8,128)S(1)} %reshape.695, f32[512,3,128]{2,1,0:T(4,128)S(1)} %reshape.696, f32[512,1,128]{2,1,0:T(1,128)} %copy.180, f32[512,128]{1,0:T(8,128)} %convert_element_type.134, f32[512,9]{1,0:T(8,128)} %copy.181, f32[512]{0:T(512)} %bitcast.188, ...), kind=kLoop, calls=%fused_computation.21.clone.1 | loop fusion | flops 4128768 | bytes 7641088 | tf_op jit(solution)/shard_map/while/body/eval_jaxpr/mul | solution.py:90
  54.4 62.4 %scatter_fusion = f32[560,9,128]{2,1,0:T(8,128)} fusion(f32[560,9,128]{2,1,0:T(8,128)} %get-tuple-element.618, s32[512]{0:T(512)S(1)} %bitcast.183, f32[512,9,128]{2,1,0:T(8,128)} %get-tuple-element.561), kind=kCustom, calls=%fused_computation.8.clone.1 | custom fusion | flops 589824 | bytes 7079936 | tf_op jit(solution)/shard_map/while/body/eval_jaxpr/scatter-add | solution.py:206
  116.8 62.3 %scatter_fusion.1 = f32[560,9,128]{2,1,0:T(8,128)} fusion(f32[560,9,128]{2,1,0:T(8,128)} %scatter_fusion, s32[512]{0:T(512)S(1)} %bitcast.181, f32[512,9,128]{2,1,0:T(8,128)} %get-tuple-element.562), kind=kCustom, calls=%fused_computation.9.clone.1 | custom fusion | flops 589824 | bytes 7079936 | tf_op jit(solution)/shard_map/while/body/eval_jaxpr/scatter-add | solution.py:206
  198.3 9.2 %fusion.207 = (f32[512,9,128]{2,1,0:T(8,128)}, f32[512,9,128]{2,1,0:T(8,128)}) fusion(f32[512,5,128]{2,1,0:T(8,128)S(1)} %reshape.695, f32[512,3,128]{2,1,0:T(4,128)S(1)} %reshape.696, f32[512,1,128]{2,1,0:T(1,128)} %copy.180, f32[512,128]{1,0:T(8,128)} %convert_element_type.134, f32[512,9]{1,0:T(8,128)} %copy.181, f32[512]{0:T(512)} %bitcast.188, ...), kind=kLoop, calls=%fused_computation.21.clone.1 | loop fusion | flops 4128768 | bytes 7641088 | tf_op jit(solution)/shard_map/while/body/eval_jaxpr/mul | solution.py:90
  207.4 62.3 %scatter_fusion = f32[560,9,128]{2,1,0:T(8,128)} fusion(f32[560,9,128]{2,1,0:T(8,128)} %get-tuple-element.618, s32[512]{0:T(512)S(1)} %bitcast.183, f32[512,9,128]{2,1,0:T(8,128)} %get-tuple-element.561), kind=kCustom, calls=%fused_computation.8.clone.1 | custom fusion | flops 589824 | bytes 7079936 | tf_op jit(solution)/shard_map/while/body/eval_jaxpr/scatter-add | solution.py:206
  269.8 62.4 %scatter_fusion.1 = f32[560,9,128]{2,1,0:T(8,128)} fusion(f32[560,9,128]{2,1,0:T(8,128)} %scatter_fusion, s32[512]{0:T(512)S(1)} %bitcast.181, f32[512,9,128]{2,1,0:T(8,128)} %get-tuple-element.562), kind=kCustom, calls=%fused_computation.9.clone.1 | custom fusion | flops 589824 | bytes 7079936 | tf_op jit(solution)/shard_map/while/body/eval_jaxpr/scatter-add | solution.py:206
  335.1 3.9 collective-permute-start.7
  339.0 4.0 slice.183
  342.9 2.8 reshape.488
  345.8 9.1 %collective-permute-done.6 = f32[1,3,3,16,1152]{4,3,2,1,0:T(8,128)} collective-permute-done((f32[1,3,3,16,1152]{4,3,2,1,0:T(8,128)}, f32[1,3,3,16,1152]{4,3,2,1,0:T(8,128)}, u32[]{:S(2)}, u32[]{:S(2)}) %collective-permute-start.6) | collective-permute-done | bytes 663584 | tf_op jit(solution)/shard_map/ppermute | solution.py:23
  356.1 10.1 %collective-permute-done.7 = f32[1,3,3,16,1152]{4,3,2,1,0:T(8,128)} collective-permute-done((f32[1,3,3,16,1152]{4,3,2,1,0:T(8,128)S(1)}, f32[1,3,3,16,1152]{4,3,2,1,0:T(8,128)}, u32[]{:S(2)}, u32[]{:S(2)}) %collective-permute-start.7) | collective-permute-done | bytes 663584 | tf_op jit(solution)/shard_map/ppermute | solution.py:24
  369.6 25.3 %collective-permute-done.9 = f32[5,1,3,16,1152]{4,3,2,1,0:T(8,128)S(1)} collective-permute-done((f32[5,1,3,16,1152]{4,3,2,1,0:T(8,128)S(1)}, f32[5,1,3,16,1152]{4,3,2,1,0:T(8,128)S(1)}, u32[]{:S(2)}, u32[]{:S(2)}) %collective-permute-start.9) | collective-permute-done | bytes 1105952 | tf_op jit(solution)/shard_map/ppermute | solution.py:24
  394.9 21.8 %collective-permute-done.8 = f32[5,1,3,16,1152]{4,3,2,1,0:T(8,128)S(1)} collective-permute-done((f32[5,1,3,16,1152]{4,3,2,1,0:T(8,128)S(1)}, f32[5,1,3,16,1152]{4,3,2,1,0:T(8,128)S(1)}, u32[]{:S(2)}, u32[]{:S(2)}) %collective-permute-start.8) | collective-permute-done | bytes 1105952 | tf_op jit(solution)/shard_map/ppermute | solution.py:23
  418.9 1.9 collective-permute-done.11
  420.8 2.6 collective-permute-done.10
  428.6 3.8 collective-permute-start.13
  432.4 1.9 collective-permute-done.12
  436.4 3.1 collective-permute-done.15
  444.7 1.8 pad_maximum_fusion.3
  447.3 165.5 %while.25 = (s32[]{:T(128)}, f32[560,128]{1,0:T(8,128)}, f32[560,3]{1,0:T(8,128)S(1)}, s32[2,512]{1,0:T(2,128)}, f32[2,512]{1,0:T(2,128)}, /*index=5*/s32[2,512]...) while((s32[]{:T(128)}, f32[560,128]{1,0:T(8,128)}, ...), condition=%wide.region_26.27_spmd.clone, body=%wide.region_10.26_spmd.sunk.clone.sunk | while | flops 372474368 | bytes 33211372 | solution.py:247
  448.3 2.7 gather_fusion.2
  465.4 2.9 gather_fusion.4
  468.3 2.0 gather_fusion.5
  471.9 21.3 %fusion.226 = (f32[512,9]{1,0:T(8,128)}, f32[512,128]{1,0:T(8,128)}, f32[512,128]{1,0:T(8,128)}, f32[512,9]{1,0:T(8,128)}, f32[512,9,128]{2,1,0:T(8,128)}) fusion(bf16[512,9,128]{2,1,0:T(8,128)(2,1)} %gather_fusion.2, f32[512,5,128]{2,1,0:T(8,128)} %reshape.713, f32[512,3,128]{2,1,0:T(4,128)} %reshape.714, f32[512,1,128]{2,1,0:T(1,128)S(1)} %copy.185, ...), kind=kLoop, calls=%fused_computation.94.clone.1 | loop fusion | flops 11656192 | bytes 8202240 | tf_op jit(solution)/shard_map/while/body/eval_jaxpr/reduce_sum | solution.py:121
  493.2 5.2 scatter_custom_fusion.23
  498.4 5.2 scatter_custom_fusion.24
  503.6 2.9 slice_reduce_fusion.9
  506.5 2.3 slice_reduce_fusion.10
  523.0 3.5 scatter_fusion.2
  526.7 3.4 scatter_fusion.3
  530.9 2.7 gather_fusion.2
  548.1 2.9 gather_fusion.4
  551.0 2.0 gather_fusion.5
  554.6 21.3 %fusion.226 = (f32[512,9]{1,0:T(8,128)}, f32[512,128]{1,0:T(8,128)}, f32[512,128]{1,0:T(8,128)}, f32[512,9]{1,0:T(8,128)}, f32[512,9,128]{2,1,0:T(8,128)}) fusion(bf16[512,9,128]{2,1,0:T(8,128)(2,1)} %gather_fusion.2, f32[512,5,128]{2,1,0:T(8,128)} %reshape.713, f32[512,3,128]{2,1,0:T(4,128)} %reshape.714, f32[512,1,128]{2,1,0:T(1,128)S(1)} %copy.185, ...), kind=kLoop, calls=%fused_computation.94.clone.1 | loop fusion | flops 11656192 | bytes 8202240 | tf_op jit(solution)/shard_map/while/body/eval_jaxpr/reduce_sum | solution.py:121
  575.9 5.2 scatter_custom_fusion.23
  581.1 5.2 scatter_custom_fusion.24
  586.2 2.9 slice_reduce_fusion.9
  589.2 2.3 slice_reduce_fusion.10
  605.6 3.5 scatter_fusion.2
  609.3 3.4 scatter_fusion.3
  613.1 3.5 collective-permute-start.19
  618.7 3.9 collective-permute-start.25
  624.7 4.0 collective-permute-done.24
  (381 shorter events, 148.9 us)
Async XLA Ops:
  0.6 15.2 %copy-start = (bf16[128,128]{1,0:T(8,128)(2,1)S(1)}, bf16[128,128]{1,0:T(8,128)(2,1)}, u32[]{:S(2)}) copy-start(bf16[128,128]{1,0:T(8,128)(2,1)} %param.28) | copy-start | bytes 98308
  0.6 25.4 %copy-start.18 = (f32[8,64]{1,0:T(8,128)S(1)}, f32[8,64]{1,0:T(8,128)}, u32[]{:S(2)}) copy-start(f32[8,64]{1,0:T(8,128)} %param.29) | copy-start | bytes 6148
  0.7 25.4 %copy-start.31 = (f32[64,64]{1,0:T(8,128)S(1)}, f32[64,64]{1,0:T(8,128)}, u32[]{:S(2)}) copy-start(f32[64,64]{1,0:T(8,128)} %param.30) | copy-start | bytes 49156
  0.7 25.4 %copy-start.1 = (f32[64,384]{1,0:T(8,128)S(1)}, f32[64,384]{1,0:T(8,128)}, u32[]{:S(2)}) copy-start(f32[64,384]{1,0:T(8,128)} %param.31) | copy-start | bytes 294916
  3.3 6.4 %collective-permute-start.1 = (bf16[1,1,1,16,128]{4,3,2,1,0:T(8,128)(2,1)S(1)}, bf16[1,1,1,16,128]{4,3,2,1,0:T(8,128)(2,1)S(1)}, u32[]{:S(2)}, u32[]{:S(2)}) collective-permute-start(bf16[1,1,1,16,128]{4,3,2,1,0:T(8,128)(2,1)S(1)} %bitcast.192), channel_id=1, source_target_pairs={{4,0},{8,4},{12,8},{0,12},{5,1},{9,5},{13,9},{1,13},{6,2},{10,6},{... | collective-permute-start | bytes 12296 | tf_op jit(solution)/shard_map/ppermute | solution.py:24
  8.4 5.4 collective-permute-start
  13.8 3.7 collective-permute-start.3
  15.3 3.7 collective-permute-start.2
  19.0 4.4 collective-permute-start.5
  19.0 4.3 collective-permute-start.4
  45.2 9.2 %copy-start.15 = (s32[512,1]{0,1:T(1,128)S(1)}, s32[512,1]{0,1:T(1,128)}, u32[]{:S(2)}) copy-start(s32[512,1]{0,1:T(1,128)} %copy-done.14) | copy-start | bytes 6148 | tf_op jit(solution)/shard_map/while
  54.4 62.4 %copy-start.13 = (s32[512,1]{0,1:T(1,128)S(1)}, s32[512,1]{0,1:T(1,128)}, u32[]{:S(2)}) copy-start(s32[512,1]{0,1:T(1,128)} %get-tuple-element.560) | copy-start | bytes 6148 | tf_op jit(solution)/shard_map/while
  116.7 62.3 %copy-start.19 = (f32[8,64]{1,0:T(8,128)S(1)}, f32[8,64]{1,0:T(8,128)}, u32[]{:S(2)}) copy-start(f32[8,64]{1,0:T(8,128)} %get-tuple-element.720) | copy-start | bytes 6148 | tf_op jit(solution)/shard_map/while
  116.8 62.3 %copy-start.32 = (f32[64,64]{1,0:T(8,128)S(1)}, f32[64,64]{1,0:T(8,128)}, u32[]{:S(2)}) copy-start(f32[64,64]{1,0:T(8,128)} %get-tuple-element.775) | copy-start | bytes 49156 | tf_op jit(solution)/shard_map/while
  198.3 9.2 %copy-start.15 = (s32[512,1]{0,1:T(1,128)S(1)}, s32[512,1]{0,1:T(1,128)}, u32[]{:S(2)}) copy-start(s32[512,1]{0,1:T(1,128)} %copy-done.14) | copy-start | bytes 6148 | tf_op jit(solution)/shard_map/while
  207.4 62.4 %copy-start.13 = (s32[512,1]{0,1:T(1,128)S(1)}, s32[512,1]{0,1:T(1,128)}, u32[]{:S(2)}) copy-start(s32[512,1]{0,1:T(1,128)} %get-tuple-element.560) | copy-start | bytes 6148 | tf_op jit(solution)/shard_map/while
  269.8 62.4 %copy-start.19 = (f32[8,64]{1,0:T(8,128)S(1)}, f32[8,64]{1,0:T(8,128)}, u32[]{:S(2)}) copy-start(f32[8,64]{1,0:T(8,128)} %get-tuple-element.720) | copy-start | bytes 6148 | tf_op jit(solution)/shard_map/while
  269.8 62.4 %copy-start.32 = (f32[64,64]{1,0:T(8,128)S(1)}, f32[64,64]{1,0:T(8,128)}, u32[]{:S(2)}) copy-start(f32[64,64]{1,0:T(8,128)} %get-tuple-element.775) | copy-start | bytes 49156 | tf_op jit(solution)/shard_map/while
  335.0 19.9 %collective-permute-start.6 = (f32[1,3,3,16,1152]{4,3,2,1,0:T(8,128)}, f32[1,3,3,16,1152]{4,3,2,1,0:T(8,128)}, u32[]{:S(2)}, u32[]{:S(2)}) collective-permute-start(f32[1,3,3,16,1152]{4,3,2,1,0:T(8,128)} %slice.182), channel_id=1, source_target_pairs={{0,4},{4,8},{8,12},{12,0},{1,5},{5,9},{9,13},{13,1},{2,6},{6,10},{... | collective-permute-start | bytes 1990664 | tf_op jit(solution)/shard_map/ppermute | solution.py:23
  335.1 31.1 %collective-permute-start.7 = (f32[1,3,3,16,1152]{4,3,2,1,0:T(8,128)S(1)}, f32[1,3,3,16,1152]{4,3,2,1,0:T(8,128)}, u32[]{:S(2)}, u32[]{:S(2)}) collective-permute-start(f32[1,3,3,16,1152]{4,3,2,1,0:T(8,128)S(1)} %slice.185), channel_id=1, source_target_pairs={{4,0},{8,4},{12,8},{0,12},{5,1},{9,5},{13,9},{1,13},{6,2},{10,6},{... | collective-permute-start | bytes 1990664 | tf_op jit(solution)/shard_map/ppermute | solution.py:24
  367.5 27.4 %collective-permute-start.9 = (f32[5,1,3,16,1152]{4,3,2,1,0:T(8,128)S(1)}, f32[5,1,3,16,1152]{4,3,2,1,0:T(8,128)S(1)}, u32[]{:S(2)}, u32[]{:S(2)}) collective-permute-start(f32[5,1,3,16,1152]{4,3,2,1,0:T(8,128)S(1)} %get-tuple-element.355), channel_id=1, source_target_pairs={{2,0},{0,2},{3,1},{1,3},{6,4},{4,6},{7,5},{5,7},{10,8},{8,10},{11,... | collective-permute-start | bytes 3317768 | tf_op jit(solution)/shard_map/ppermute | solution.py:24
  368.1 49.4 %copy-start.30 = (f32[3,128]{1,0:T(4,128)S(1)}, f32[3,128]{1,0:T(4,128)}, u32[]{:S(2)}) copy-start(f32[3,128]{1,0:T(4,128)} %param.32) | copy-start | bytes 4612
  368.2 48.5 %collective-permute-start.8 = (f32[5,1,3,16,1152]{4,3,2,1,0:T(8,128)S(1)}, f32[5,1,3,16,1152]{4,3,2,1,0:T(8,128)S(1)}, u32[]{:S(2)}, u32[]{:S(2)}) collective-permute-start(f32[5,1,3,16,1152]{4,3,2,1,0:T(8,128)S(1)} %get-tuple-element.354), channel_id=1, source_target_pairs={{0,2},{2,0},{1,3},{3,1},{4,6},{6,4},{5,7},{7,5},{8,10},{10,8},{9,1... | collective-permute-start | bytes 3317768 | tf_op jit(solution)/shard_map/ppermute | solution.py:23
  417.0 3.9 collective-permute-start.11
  417.0 6.4 %collective-permute-start.10 = (f32[5,5,1,16,1152]{4,3,2,1,0:T(8,128)S(1)}, f32[5,5,1,16,1152]{4,3,2,1,0:T(8,128)S(1)}, u32[]{:S(2)}, u32[]{:S(2)}) collective-permute-start(f32[5,5,1,16,1152]{4,3,2,1,0:T(8,128)S(1)} %get-tuple-element.350), channel_id=1, source_target_pairs={{0,1},{1,0},{2,3},{3,2},{4,5},{5,4},{6,7},{7,6},{8,9},{9,8},{10,11... | collective-permute-start | bytes 5529608 | tf_op jit(solution)/shard_map/ppermute | solution.py:23
  428.5 5.8 collective-permute-start.12
  428.6 5.8 collective-permute-start.13
  434.3 5.2 collective-permute-start.15
  435.0 5.7 collective-permute-start.14
  440.8 1.7 collective-permute-start.17
  440.9 2.1 collective-permute-start.16
  448.2 10.5 %copy-start.11 = (s32[512,1]{0,1:T(1,128)}, s32[512,1]{0,1:T(1,128)S(1)}, u32[]{:S(2)}) copy-start(s32[512,1]{0,1:T(1,128)S(1)} %get-tuple-element.575) | copy-start | bytes 6148 | tf_op jit(solution)/shard_map/while
  515.2 11.4 %copy-start.10 = (s32[512,1]{0,1:T(1,128)S(1)}, s32[512,1]{0,1:T(1,128)}, u32[]{:S(2)}) copy-start(s32[512,1]{0,1:T(1,128)} %copy-done.9) | copy-start | bytes 6148 | tf_op jit(solution)/shard_map/while
  530.9 10.5 %copy-start.11 = (s32[512,1]{0,1:T(1,128)}, s32[512,1]{0,1:T(1,128)S(1)}, u32[]{:S(2)}) copy-start(s32[512,1]{0,1:T(1,128)S(1)} %get-tuple-element.575) | copy-start | bytes 6148 | tf_op jit(solution)/shard_map/while
  597.9 11.4 %copy-start.10 = (s32[512,1]{0,1:T(1,128)S(1)}, s32[512,1]{0,1:T(1,128)}, u32[]{:S(2)}) copy-start(s32[512,1]{0,1:T(1,128)} %copy-done.9) | copy-start | bytes 6148 | tf_op jit(solution)/shard_map/while
  612.8 23.1 %copy-start.28 = (s32[16]{0:T(128)S(1)}, s32[16]{0:T(128)}, u32[]{:S(2)}) copy-start(s32[16]{0:T(128)} %copy-done.26) | copy-start | bytes 196
  613.1 9.5 %collective-permute-start.19 = (f32[1,3,3,3,16]{4,2,1,0,3:T(4,128)S(1)}, f32[1,3,3,3,16]{4,2,1,0,3:T(4,128)S(1)}, u32[]{:S(2)}, u32[]{:S(2)}) collective-permute-start(f32[1,3,3,3,16]{4,2,1,0,3:T(4,128)S(1)} %get-tuple-element.367), channel_id=1, source_target_pairs={{4,0},{8,4},{12,8},{0,12},{5,1},{9,5},{13,9},{1,13},{6,2},{10,6},{... | collective-permute-start | bytes 5192 | tf_op jit(solution)/shard_map/ppermute | solution.py:24
  616.6 6.0 collective-permute-start.18
  618.7 6.0 collective-permute-start.25
  622.6 6.2 collective-permute-start.24
  622.7 10.5 %collective-permute-start.21 = (f32[5,1,3,3,16]{4,3,2,1,0:T(4,128)S(1)}, f32[5,1,3,3,16]{4,3,2,1,0:T(4,128)S(1)}, u32[]{:S(2)}, u32[]{:S(2)}) collective-permute-start(f32[5,1,3,3,16]{4,3,2,1,0:T(4,128)S(1)} %get-tuple-element.365), channel_id=1, source_target_pairs={{2,0},{0,2},{3,1},{1,3},{6,4},{4,6},{7,5},{5,7},{10,8},{8,10},{11,... | collective-permute-start | bytes 8648 | tf_op jit(solution)/shard_map/ppermute | solution.py:24
  623.4 9.7 %collective-permute-start.20 = (f32[5,1,3,3,16]{4,3,2,1,0:T(4,128)S(1)}, f32[5,1,3,3,16]{4,3,2,1,0:T(4,128)S(1)}, u32[]{:S(2)}, u32[]{:S(2)}) collective-permute-start(f32[5,1,3,3,16]{4,3,2,1,0:T(4,128)S(1)} %get-tuple-element.364), channel_id=1, source_target_pairs={{0,2},{2,0},{1,3},{3,1},{4,6},{6,4},{5,7},{7,5},{8,10},{10,8},{9,1... | collective-permute-start | bytes 8648 | tf_op jit(solution)/shard_map/ppermute | solution.py:23
  628.8 5.0 collective-permute-start.27
  629.6 5.5 collective-permute-start.26
  633.2 2.4 collective-permute-start.23
  633.3 2.4 collective-permute-start.22
  635.1 2.2 collective-permute-start.29
  635.1 2.1 collective-permute-start.28
  (44 other events, 191.8 us)
where the time goes:
time: 647 us; the launch traced here: 639 us
  other arithmetic  395 us (61%)
  local copies, waits for them, and re-layouts  97.5 us (15%)
  waiting for transfers between devices  91.6 us (14%)
  starting transfers between devices  33.4 us (5%)
  matrix products  18.4 us (3%)
    scatter-add x4, other arithmetic, gather_step(): amp_table.at[first_rows].add(toward_first).at[second_rows]  249 us
    ppermute x15, waiting for transfers between devices, padded(): before = lax.ppermute(last, axis, up)  47.9 us
    ppermute x15, waiting for transfers between devices, padded(): after = lax.ppermute(first, axis, down)  43.7 us
    reduce_sum x2, other arithmetic, pair_gradients(): jnp.sum(second_grad * spread * first_up[:, None, :], axis=2)  42.6 us
    ppermute x15, starting transfers between devices, padded(): after = lax.ppermute(first, axis, down)  24.9 us
    scatter-add x4, other arithmetic, grad_step(): up_table.at[first_rows].add(up_first).at[second_rows].add(up_second)  20.7 us
    mul x2, other arithmetic, pair_messages(): spread * (harmonic * parity)[:, :, None] * first_up[:, None, :]  18.3 us
    scatter-add x4, other arithmetic, grad_step(): force_table.at[first_rows].add(grad_vectors).at[second_rows]  13.9 us
  transfers between devices with their start and end apart: 30, of which 17 were waited for; matrix products, arithmetic and copies ran while one was open for 3% of the time, Pallas kernels for 0%

commit v1 on v0

v1 whole, which is shorter than its diff:
```python
import functools
import math

import jax
import jax.numpy as jnp
from jax import lax
from jax.experimental import pallas as pl
from jax.experimental.pallas import tpu as pltpu
from jax.sharding import PartitionSpec as P

CUTOFF = 5.0
S3 = math.sqrt(3.0)
S5 = math.sqrt(5.0)
S15 = math.sqrt(15.0)
F32 = jnp.float32
BF16 = jnp.bfloat16
MESH = pl.DeviceIdType.MESH
DEGREE_ROWS = ((0, 1), (1, 4), (4, 9))


def nn(a, b):
    return lax.dot_general(a, b, (((1,), (0,)), ((), ())), preferred_element_type=F32)


def nt(a, b):
    return lax.dot_general(a, b, (((1,), (1,)), ((), ())), preferred_element_type=F32)


def rounded(x):
    return x.astype(BF16).astype(F32)


def split_weights(w):
    depth, width = w.shape
    hi = rounded(w)
    stack = jnp.concatenate([hi, hi, w - hi], axis=0)
    rows = -(-3 * depth // 128) * 128
    stack = jnp.concatenate([stack, jnp.zeros((rows - 3 * depth, width), F32)], axis=0)
    columns = -(-width // 128) * 128
    if columns > width:
        stack = jnp.concatenate([stack, jnp.zeros((rows, columns - width), F32)], axis=1)
    return jnp.transpose(stack)[:width].astype(BF16)


def split_values(h, rows):
    hi = rounded(h)
    parts = [hi, h - hi, hi]
    spare = rows - 3 * h.shape[0]
    if spare:
        parts.append(jnp.zeros((spare, h.shape[1]), F32))
    return jnp.concatenate(parts, axis=0).astype(BF16)


def flipped(w):
    return jnp.transpose(w.astype(F32)).astype(BF16)


def polynomial(x, coefficients):
    total = coefficients[-1]
    for c in coefficients[-2::-1]:
        total = total * x + c
    return total


SIN_SERIES = [(-1.0) ** i / math.factorial(2 * i + 1) for i in range(7)]
COS_SERIES = [(-1.0) ** i / math.factorial(2 * i) for i in range(8)]


def direction(vx, vy, vz):
    square = vx * vx + vy * vy + vz * vz
    inverse = lax.rsqrt(square)
    return square * inverse, inverse, (vx * inverse, vy * inverse, vz * inverse)


def radial_network(distance, inverse, orders, one, two, three):
    lanes = distance.shape[1]
    x = distance * (1.0 / CUTOFF)
    phase = math.pi * x - 0.5 * math.pi
    square = phase * phase
    sine = polynomial(square, COS_SERIES)
    cosine = -phase * polynomial(square, SIN_SERIES)
    sines, cosines = [sine], [cosine]
    for _ in range(orders - 1):
        s, c = sines[-1], cosines[-1]
        sines.append(s * cosine + c * sine)
        cosines.append(c * cosine - s * sine)
    x2 = x * x
    x5 = x2 * x2 * x
    envelope = 1.0 - x5 * x * (28.0 - 48.0 * x + 21.0 * x2)
    slope = -168.0 * x5 * (1.0 - x) * (1.0 - x)
    scale = math.sqrt(2.0 / CUTOFF) * inverse
    factor = scale * envelope
    factor_slope = scale * (slope * (1.0 / CUTOFF) - envelope * inverse)
    sin_rows = jnp.concatenate(sines, axis=0)
    cos_rows = jnp.concatenate(cosines, axis=0)
    number = lax.broadcasted_iota(jnp.int32, (orders, lanes), 0).astype(F32) + 1.0
    basis = sin_rows * factor
    basis_slope = cos_rows * (number * (math.pi / CUTOFF)) * factor + sin_rows * factor_slope
    both = jnp.concatenate([basis, basis_slope], axis=1)
    for weights in (one, two):
        both = nn(weights, split_values(both, weights.shape[1]))
        value, tangent = both[:, :lanes], both[:, lanes:]
        sigmoid = jax.nn.sigmoid(value)
        hidden = value * sigmoid
        tangent = tangent * (sigmoid + hidden * (1.0 - sigmoid))
        both = jnp.concatenate([hidden, tangent], axis=1)
    both = nn(three, split_values(both, three.shape[1]))
    return both[:, :lanes], both[:, lanes:]


def harmonic_rows(n, w):
    x, y, z = n
    wx, wy, wz = (w * x, w * y, w * z)
    return (
        w,
        S3 * wx,
        S3 * wy,
        S3 * wz,
        S15 * wx * z,
        S15 * wx * y,
        S5 * (wy * y - 0.5 * (wx * x + wz * z)),
        S15 * wy * z,
        0.5 * S15 * (wz * z - wx * x),
    )


class Plan:
    def __init__(self, sizes, slots):
        self.sizes = sizes
        self.slots = slots
        self.classes = tuple(2 if n == 2 else 3 for n in sizes)
        self.subs = tuple(2 if n == 2 else 1 for n in sizes)
        self.count = math.prod(self.classes)
        self.members = [[] for _ in range(self.count)]
        self.sub_of = {}
        for g in range(27):
            o = (g // 9, g // 3 % 3, g % 3)
            index, sub = self.index(o), self.sub(o)
            self.members[index].append(g)
            self.sub_of[g] = sub
        self.own = self.index((1, 1, 1))
        self.others = [d for d in range(self.count) if d != self.own]
        self.start, self.rows, self.block_start = {}, {}, {}
        total = 0
        for d in self.others:
            self.start[d] = total
            self.rows[d] = slots * (2 + len(self.members[d]))
            for i, g in enumerate(self.members[d]):
                self.block_start[g] = total + slots * (2 + i)
            total += self.rows[d]
        self.total = total

    def index(self, o, turned=False):
        value = 0
        for part, n, classes in zip(o, self.sizes, self.classes):
            part = part & 1 if n == 2 else (2 - part if turned else part)
            value = value * classes + part
        return value

    def sub(self, o):
        value = 0
        for part, n, subs in zip(o, self.sizes, self.subs):
            value = value * subs + (part >> 1 if n == 2 else part * 0)
        return value

    def class_of_block(self, g):
        return self.index((g // 9, g // 3 % 3, g % 3))

    def shift(self, d):
        out = []
        for classes in reversed(self.classes):
            out.append(d % classes - 1)
            d //= classes
        return tuple(reversed(out))

    def lane_offsets(self, g):
        a = (g * 57) >> 9
        rest = g - 9 * a
        b = (rest * 11) >> 5
        return (a, b, rest - 3 * b)


def kernel(
    plan,
    feats_ref,
    species_ref,
    export_ref,
    first_ref,
    second_ref,
    live_ref,
    disp_ref,
    w_up_ref,
    one_ref,
    two_ref,
    three_ref,
    power_ref,
    w_mix_ref,
    read_ref,
    base_ref,
    energy_ref,
    force_ref,
    grad_ref,
    send_one,
    recv_one,
    send_two,
    recv_two,
    edge_in,
    info_in,
    ghost_in,
    radial_ref,
    slope_ref,
    up_ref,
    m_ref,
    s_ref,
    hot_one,
    hot_two,
    hot_back,
    hot_ghost,
    g_wide,
    g_tall,
    s1,
    r1,
    s2,
    r2,
):
    atoms, channels = feats_ref.shape
    pairs = first_ref.shape[1]
    slots = plan.slots
    head = pairs - 27 * slots
    cut = head // 128 * 128
    width = pairs - cut
    pad = head - cut
    orders = one_ref.shape[0]
    norm = 1.0 / math.sqrt(2.0 * pairs / atoms)

    me = tuple(lax.axis_index(a) for a in ("groups", "gx", "gy", "gz"))

    def device(d, turn):
        place = [me[0]]
        for here, step, n in zip(me[1:], plan.shift(d), plan.sizes):
            place.append(lax.rem(here + turn * step + n, n))
        return tuple(place)

    barrier = pltpu.get_barrier_semaphore()
    for d in plan.others:
        pl.semaphore_signal(barrier, inc=1, device_id=device(d, 1), device_id_type=MESH)

    lane = lax.broadcasted_iota(jnp.int32, (1, width), 1)
    block = jnp.maximum(lane - pad, 0) >> 4
    offsets = plan.lane_offsets(block)
    own_lane = jnp.logical_or(lane < pad, block == 13)
    lane_sub = plan.sub(offsets)
    ghost_base = plan.index(offsets, turned=True) * slots

    first = first_ref[...]
    second = second_ref[...]
    live = live_ref[...].astype(F32)
    vx, vy, vz = disp_ref[0:1, :], disp_ref[1:2, :], disp_ref[2:3, :]

    atom_row = lax.broadcasted_iota(jnp.int32, (atoms, pairs), 0)
    hot_one[...] = (atom_row == first).astype(F32).astype(BF16)
    hot_two[...] = (atom_row == second).astype(F32).astype(BF16)
    export_hot = (
        (lax.broadcasted_iota(jnp.int32, (atoms, slots), 0) == export_ref[...])
        .astype(F32)
        .astype(BF16)
    )
    feats = feats_ref[...]

    window_slot = (second[:, cut:] - atoms) & (slots - 1)
    rows16 = []
    for v in (vx, vy, vz):
        piece = v[:, cut:]
        for _ in range(3):
            hi = rounded(piece)
            rows16.append(hi)
            piece = piece - hi
    rows16.append(live[:, cut:])
    rows16.append(window_slot.astype(F32))
    rows16.append(jnp.zeros((16 - len(rows16), width), F32))
    group16 = jnp.concatenate(rows16, axis=0)
    tall_group = lax.broadcasted_iota(jnp.int32, (128, width), 0) >> 4
    tiled = jnp.concatenate([group16] * 8, axis=0)
    info_rows = jnp.transpose(jnp.where(tall_group == lane_sub, tiled, 0.0))

    def transposed_dot(a, b):
        return nn(jnp.transpose(a.astype(F32)).astype(BF16), b)

    first_rows = transposed_dot(hot_one[:, cut:], feats).astype(BF16)
    offered = transposed_dot(
        jnp.concatenate([export_hot.astype(F32), jnp.zeros((atoms, 128 - slots), F32)], axis=1),
        feats,
    )[:slots].astype(BF16)
    for d in plan.others:
        at = plan.start[d]
        send_one[at : at + slots, :] = offered
        tile = None
        for g in plan.members[d]:
            part = info_rows[pad + slots * g : pad + slots * (g + 1), :]
            tile = part if tile is None else tile + part
            spot = plan.block_start[g]
            send_one[spot : spot + slots, :] = first_rows[pad + slots * g : pad + slots * (g + 1), :]
        send_one[at + slots : at + 2 * slots, :] = tile.astype(BF16)

    pl.semaphore_wait(barrier, len(plan.others))
    first_copies = []
    for d in plan.others:
        part = pl.ds(plan.start[d], plan.rows[d])
        copy = pltpu.make_async_remote_copy(
            src_ref=send_one.at[part],
            dst_ref=recv_one.at[part],
            send_sem=s1.at[d],
            recv_sem=r1.at[d],
            device_id=device(d, 1),
            device_id_type=MESH,
        )
        copy.start()
        first_copies.append(copy)

    one = split_weights(one_ref[...])
    two = split_weights(two_ref[...])
    three = split_weights(three_ref[...])
    w_up = w_up_ref[...]
    w_up_t = flipped(w_up)
    w_mix = w_mix_ref[...]
    w_mix_t = flipped(w_mix)
    tables = jnp.transpose(
        jnp.concatenate(
            [
                power_ref[...],
                read_ref[...],
                jnp.zeros((128 - 3 - read_ref.shape[0], channels), F32),
            ],
            axis=0,
        )
    )
    up_t = nt(w_up_t, feats).astype(BF16)

    weight = live * norm
    edges = []

    def geometry(ax, ay, az, at):
        distance, inverse, n = direction(ax, ay, az)
        radial, slope = radial_network(distance, inverse, orders, one, two, three)
        lanes = ax.shape[1]
        radial_ref[:, at : at + lanes] = radial
        slope_ref[:, at : at + lanes] = slope
        return inverse, n

    def scaled_hot(hot, rows, at):
        hot = hot.astype(F32)
        lanes = hot.shape[1]
        for k in range(9):
            s_ref[k * atoms : (k + 1) * atoms, at : at + lanes] = (hot * rows[k]).astype(BF16)

    def messages(radial_at, up, at):
        lanes = up.shape[1]
        up_ref[:, at : at + lanes] = up.astype(BF16)
        for l in range(3):
            here = slice(l * channels, (l + 1) * channels)
            m_ref[here, at : at + lanes] = (
                radial_ref[here, radial_at : radial_at + lanes] * up
            ).astype(BF16)

    inverse_a, n_a = [], []
    for at in (0, cut):
        part = slice(at, at + width) if at else slice(0, cut)
        inverse, n = geometry(vx[:, part], vy[:, part], vz[:, part], part.start)
        inverse_a.append(inverse)
        n_a.append(n)
        scaled_hot(hot_one[:, part], harmonic_rows(n, weight[:, part]), part.start)
    turned_low = tuple(-x for x in n_a[0])
    scaled_hot(hot_two[:, :cut], harmonic_rows(turned_low, weight[:, :cut]), pairs)
    messages(0, nn(up_t, hot_two[:, :cut]), 0)
    messages(0, nn(up_t, hot_one[:, :cut]), pairs)
    ghost_row = lax.broadcasted_iota(jnp.int32, (plan.count * slots, width), 0)
    ghost_at = jnp.where(own_lane, -1, ghost_base + window_slot)
    hot_ghost[...] = (ghost_row == ghost_at).astype(F32).astype(BF16)
    edge_in[...] = first_rows
    info_in[...] = jnp.zeros((width, 128), BF16)
    ghost_in[...] = jnp.zeros((plan.count * slots, channels), BF16)

    for copy in first_copies:
        copy.wait()
    for d in plan.others:
        at = plan.start[d]
        ghost_in[d * slots : (d + 1) * slots, :] = recv_one[at : at + slots, :]
        tile = recv_one[at + slots : at + 2 * slots, :]
        for g in plan.members[d]:
            spot = plan.block_start[g]
            here = slice(pad + slots * g, pad + slots * (g + 1))
            edge_in[here, :] = recv_one[spot : spot + slots, :]
            info_in[here, :] = tile

    row = lax.broadcasted_iota(jnp.int32, (width, 128), 0)
    row_block = jnp.maximum(row - pad, 0) >> 4
    row_sub = plan.sub(plan.lane_offsets(row_block))
    column = lax.broadcasted_iota(jnp.int32, (width, 128), 1) >> 4
    info_own = jnp.where(column == row_sub, info_in[...].astype(F32), 0.0).astype(BF16)
    pick_row = lax.broadcasted_iota(jnp.int32, (16, 128), 0)
    pick_at = lax.broadcasted_iota(jnp.int32, (16, 128), 1) & 15
    pick = jnp.where(pick_at < 9, (pick_at * 11) >> 5, pick_at - 6) == pick_row
    incoming = nt(pick.astype(F32).astype(BF16), info_own)
    slot_in = incoming[4:5, :].astype(jnp.int32)
    slot_hot = (lax.broadcasted_iota(jnp.int32, (slots, width), 0) == slot_in).astype(F32)
    export_rows = jnp.broadcast_to(export_ref[...].astype(F32), (8, slots))
    target = nn(export_rows.astype(BF16), slot_hot.astype(BF16))[0:1, :].astype(jnp.int32)
    target = jnp.where(own_lane, second[:, cut:], target)
    weight_b = jnp.where(own_lane, live[:, cut:], incoming[3:4, :]) * norm
    back = []
    for i, v in enumerate((vx, vy, vz)):
        back.append(-jnp.where(own_lane, v[:, cut:], incoming[i : i + 1, :]))
    hot_b = (lax.broadcasted_iota(jnp.int32, (atoms, width), 0) == target).astype(F32)
    hot_back[...] = hot_b.astype(BF16)
    inverse_b, n_b = geometry(*back, pairs)
    scaled_hot(hot_b, harmonic_rows(n_b, weight_b), pairs + cut)
    ghost_up = nt(w_up_t, ghost_in[...]).astype(BF16)
    messages(cut, nn(up_t, hot_two[:, cut:]) + nn(ghost_up, hot_ghost[...]), cut)
    messages(pairs, rounded(nt(w_up_t, edge_in[...])), pairs + cut)

    amps = []
    for l, (low, high) in enumerate(DEGREE_ROWS):
        sums = nt(m_ref[l * channels : (l + 1) * channels, :], s_ref[low * atoms : high * atoms, :])
        amps += [sums[:, i * atoms : (i + 1) * atoms] for i in range(high - low)]
    power = [tables[:, l : l + 1] for l in range(3)]
    product = amps[0]
    for l, (low, high) in enumerate(DEGREE_ROWS):
        total = amps[low] * amps[low]
        for k in range(low + 1, high):
            total = total + amps[k] * amps[k]
        product = product + power[l] * total
    mixed = nn(w_mix_t, product.astype(BF16))
    species = species_ref[...]
    picker = (lax.broadcasted_iota(jnp.int32, (128, atoms), 0) == species + 3).astype(F32)
    read_rows = lax.dot_general(
        tables,
        picker,
        (((1,), (0,)), ((), ())),
        precision=lax.Precision.HIGHEST,
        preferred_element_type=F32,
    )
    base = jnp.zeros((1, atoms), F32)
    for s in range(read_ref.shape[0]):
        base = base + jnp.where(species == s, base_ref[s], 0.0)
    sigmoid = jax.nn.sigmoid(mixed)
    energy_ref[...] = jnp.sum(mixed * sigmoid * read_rows, axis=0, keepdims=True) + base
    grad_mixed = (read_rows * sigmoid * (1.0 + mixed * (1.0 - sigmoid))).astype(BF16)
    grad_product = nn(w_mix, grad_mixed)
    for l, (low, high) in enumerate(DEGREE_ROWS):
        twice = grad_product * (2.0 * power[l])
        for k in range(low, high):
            value = twice * amps[k]
            if k == 0:
                value = value + grad_product
            value = value.astype(BF16)
            g_wide[:, k * atoms : (k + 1) * atoms] = value
            g_tall[k * channels : (k + 1) * channels, :] = value

    def backward(at, radial_at, hot, n, inverse, w):
        lanes = hot.shape[1]
        here = slice(at, at + lanes)
        there = slice(radial_at, radial_at + lanes)
        source, along = 0.0, 0.0
        for l, (low, high) in enumerate(DEGREE_ROWS):
            held = nn(g_wide[:, low * atoms : high * atoms], s_ref[low * atoms : high * atoms, here])
            part = slice(l * channels, (l + 1) * channels)
            source = source + radial_ref[part, there] * held
            along = along + slope_ref[part, there] * held
        along = jnp.sum(along * up_ref[:, here].astype(F32), axis=0, keepdims=True)
        p = [None]
        for k in range(1, 9):
            l = 1 if k < 4 else 2
            gathered = nn(g_tall[k * channels : (k + 1) * channels, :], hot)
            values = m_ref[l * channels : (l + 1) * channels, here].astype(F32)
            p.append(jnp.sum(gathered * values, axis=0, keepdims=True))
        x, y, z = n
        dx = S3 * p[1] + S15 * (z * p[4] + y * p[5] - x * p[8]) - S5 * x * p[6]
        dy = S3 * p[2] + S15 * (x * p[5] + z * p[7]) + 2.0 * S5 * y * p[6]
        dz = S3 * p[3] + S15 * (x * p[4] + y * p[7] + z * p[8]) - S5 * z * p[6]
        scale = w * inverse
        radial_part = along - scale * (x * dx + y * dy + z * dz)
        g = (
            scale * dx + x * radial_part,
            scale * dy + y * radial_part,
            scale * dz + z * radial_part,
        )
        hi = [rounded(v) for v in g]
        lo = [v - h for v, h in zip(g, hi)]
        fill = jnp.zeros((10, lanes), F32)
        return source, jnp.concatenate(list(g) + [jnp.zeros((13, lanes), F32)], axis=0), (
            jnp.concatenate(hi + lo + [fill], axis=0).astype(BF16)
        )

    source_a, _, split_a = backward(
        cut, cut, hot_one[:, cut:], n_a[1], inverse_a[1], weight[:, cut:]
    )
    source_b, force_b, split_b = backward(
        pairs + cut, pairs, hot_back[...], n_b, inverse_b, weight_b
    )
    source_a = source_a.astype(BF16)
    ghost_grad = nt(hot_ghost[...], source_a)
    ghost_force = -nt(
        hot_ghost[...],
        jnp.concatenate([split_a.astype(F32), jnp.zeros((112, width), F32)], axis=0).astype(BF16),
    )
    edge_grad = jnp.transpose(source_b).astype(BF16)
    tiled = jnp.concatenate([-force_b] * 8, axis=0)
    edge_force = jnp.transpose(jnp.where(tall_group == lane_sub + 1, tiled, 0.0))
    second_copies = []
    for d in plan.others:
        at = plan.start[d]
        ghost = slice(d * slots, (d + 1) * slots)
        send_two[at : at + slots, :] = ghost_grad[ghost, :].astype(BF16)
        tile = ghost_force[ghost, :]
        for g in plan.members[d]:
            here = slice(pad + slots * g, pad + slots * (g + 1))
            tile = tile + edge_force[here, :]
            spot = plan.block_start[g]
            send_two[spot : spot + slots, :] = edge_grad[here, :]
        send_two[at + slots : at + 2 * slots, :] = tile.astype(BF16)
        part = pl.ds(at, plan.rows[d])
        copy = pltpu.make_async_remote_copy(
            src_ref=send_two.at[part],
            dst_ref=recv_two.at[part],
            send_sem=s2.at[d],
            recv_sem=r2.at[d],
            device_id=device(d, -1),
            device_id_type=MESH,
        )
        copy.start()
        second_copies.append(copy)

    source_c, _, split_c = backward(0, 0, hot_one[:, :cut], n_a[0], inverse_a[0], weight[:, :cut])
    source_d, _, split_d = backward(
        pairs, 0, hot_two[:, :cut], turned_low, inverse_a[0], weight[:, :cut]
    )
    grad_up = (
        nt(hot_two[:, cut:], source_a)
        + nt(hot_two[:, :cut], source_c.astype(BF16))
        + nt(hot_one[:, :cut], source_d.astype(BF16))
    )
    force = nt(split_a, hot_one[:, cut:]) - nt(split_a, hot_two[:, cut:])
    force = force + nt(split_b, hot_back[...])
    force = force + nt(split_c, hot_one[:, :cut]) - nt(split_c, hot_two[:, :cut])
    force = force + nt(split_d, hot_two[:, :cut]) - nt(split_d, hot_one[:, :cut])
    edge_in[...] = edge_grad
    info_in[...] = edge_force.astype(BF16)

    for copy in second_copies:
        copy.wait()
    offered_grad, offered_force = 0.0, 0.0
    for d in plan.others:
        at = plan.start[d]
        offered_grad = offered_grad + recv_two[at : at + slots, :].astype(F32)
        tile = recv_two[at + slots : at + 2 * slots, :]
        offered_force = offered_force + tile.astype(F32)
        for g in plan.members[d]:
            spot = plan.block_start[g]
            here = slice(pad + slots * g, pad + slots * (g + 1))
            edge_in[here, :] = recv_two[spot : spot + slots, :]
            info_in[here, :] = tile
    info_own = jnp.where(column == row_sub + 1, info_in[...].astype(F32), 0.0).astype(BF16)
    offered_column = lax.broadcasted_iota(jnp.int32, (slots, 128), 1)
    offered_force = jnp.where(offered_column < 16, offered_force, 0.0)
    window_hot = hot_one[:, cut:]
    grad_up = grad_up + nn(window_hot, edge_in[...]) + nn(export_hot, offered_grad.astype(BF16))
    remote_force = nn(window_hot, info_own) + nn(export_hot, offered_force.astype(BF16))
    remote_force = jnp.transpose(remote_force)
    total = force[0:3, :] + force[3:6, :]
    for j in range(8):
        total = total + remote_force[16 * j : 16 * j + 3, :] + remote_force[16 * j + 3 : 16 * j + 6, :]
    force_ref[...] = total
    grad_ref[...] = nt(grad_up.astype(BF16), w_up).astype(BF16)


def on_device(plan, *args):
    (
        node_feats,
        species,
        export_index,
        pair_first,
        pair_second,
        pair_live,
        displacement,
        w_up,
        radial_one,
        radial_two,
        radial_three,
        power_weight,
        w_mix,
        read_table,
        base_energy,
    ) = args
    atoms, channels = node_feats.shape
    pairs = pair_first.shape[0]
    slots = export_index.shape[0]
    cut = (pairs - 27 * slots) // 128 * 128
    width = pairs - cut
    ghosts = plan.count * slots
    vmem = pl.BlockSpec(memory_space=pltpu.VMEM)
    smem = pl.BlockSpec(memory_space=pltpu.SMEM)
    energy, forces, grad = pl.pallas_call(
        functools.partial(kernel, plan),
        out_shape=(
            jax.ShapeDtypeStruct((1, atoms), F32),
            jax.ShapeDtypeStruct((3, atoms), F32),
            jax.ShapeDtypeStruct((atoms, channels), BF16),
        ),
        in_specs=[vmem] * 14 + [smem],
        out_specs=(vmem,) * 3,
        scratch_shapes=[pltpu.VMEM((plan.total, channels), BF16)] * 4
        + [
            pltpu.VMEM((width, channels), BF16),
            pltpu.VMEM((width, 128), BF16),
            pltpu.VMEM((ghosts, channels), BF16),
            pltpu.VMEM((3 * channels, pairs + width), F32),
            pltpu.VMEM((3 * channels, pairs + width), F32),
            pltpu.VMEM((channels, 2 * pairs), BF16),
            pltpu.VMEM((3 * channels, 2 * pairs), BF16),
            pltpu.VMEM((9 * atoms, 2 * pairs), BF16),
            pltpu.VMEM((atoms, pairs), BF16),
            pltpu.VMEM((atoms, pairs), BF16),
            pltpu.VMEM((atoms, width), BF16),
            pltpu.VMEM((ghosts, width), BF16),
            pltpu.VMEM((channels, 9 * atoms), BF16),
            pltpu.VMEM((9 * channels, atoms), BF16),
        ]
        + [pltpu.SemaphoreType.DMA((plan.count,))] * 4,
        compiler_params=pltpu.CompilerParams(
            collective_id=0, has_side_effects=True, vmem_limit_bytes=48 * 1024 * 1024
        ),
    )(
        node_feats,
        species.reshape(1, atoms),
        export_index.reshape(1, slots),
        pair_first.reshape(1, pairs),
        pair_second.reshape(1, pairs),
        pair_live.reshape(1, pairs),
        displacement,
        w_up,
        radial_one,
        radial_two,
        radial_three,
        power_weight,
        w_mix,
        read_table,
        base_energy,
    )
    return energy.reshape(atoms), forces, grad


def solution(mesh):
    every = ("groups", "gx", "gy", "gz")
    plan = Plan(tuple(mesh.shape[a] for a in ("gx", "gy", "gz")), 16)
    in_specs = (
        (P(every, None),) + (P(every),) * 5 + (P(None, every),) + (P(),) * 8
    )
    out_specs = (P(every), P(None, every), P(every, None))
    return jax.shard_map(
        functools.partial(on_device, plan),
        mesh=mesh,
        in_specs=in_specs,
        out_specs=out_specs,
        check_vma=False,
    )
```

time: 647 us -> 33.5 us (0.05); the launches traced: 639 us -> 32.9 us
  other arithmetic: 395 us -> 0 us
  waiting for transfers between devices: 91.6 us -> 0 us
  local copies, waits for them, and re-layouts: 97.5 us -> 10.4 us
  starting transfers between devices: 33.4 us -> 0 us
  Pallas kernels: 0 us -> 21.8 us
  matrix products: 18.4 us -> 0 us
    scatter-add x15 -> x0, other arithmetic: 286 us -> none  [the longest x4 249 us: gather_step(): amp_table.at[first_rows].add(toward_first).at[second_rows]]
    ppermute x30 -> x0, waiting for transfers between devices: 91.6 us -> none  [the longest x15 47.9 us: padded(): before = lax.ppermute(last, axis, up)]
    reduce_sum x17 -> x0, other arithmetic: 58 us -> none  [the longest x2 42.6 us: pair_gradients(): jnp.sum(second_grad * spread * first_up[:, None, :], axis=2)]
    ppermute x30 -> x0, starting transfers between devices: 33.4 us -> none  [the longest x15 24.9 us: padded(): after = lax.ppermute(first, axis, down)]
    gather x14 -> x0, local copies, waits for them, and re-layouts: 25.6 us -> none  [the longest x2 5.78 us: grad_step(): node_grad[first_rows].astype(jnp.float32)]
    mul x20 -> x0, other arithmetic: 25.6 us -> none  [the longest x2 18.3 us: pair_messages(): spread * (harmonic * parity)[:, :, None] * first_up[:, None, :]]
    slice x28 -> x0, local copies, waits for them, and re-layouts: 22 us -> none  [the longest x1 3.99 us: on_device(): amps_nodes[atom_count:].reshape(3, 3, 3, slot_count, 9 * channels)]
    pallas_call x0 -> x1, Pallas kernels: none -> 21.8 us  [on_device(): pl.pallas_call(functools.partial(kernel, plan), out_shape=(jax.ShapeDtype...]
  transfers between devices with their start and end apart: 30 -> 0, of which waited for: 17 -> 0; matrix products, arithmetic and copies ran while one was open for 3% -> 0% of each run, Pallas kernels for 0% -> 0%
where the time goes in v1:
time: 33.5 us; the launch traced here: 32.9 us
  Pallas kernels  21.8 us (65%)
  local copies, waits for them, and re-layouts  10.4 us (31%)
  between operations  0.69 us (2%)
    pallas_call x1, Pallas kernels, on_device(): pl.pallas_call(functools.partial(kernel, plan), out_shape=(jax.ShapeDtype...  21.8 us
    unnamed x33, local copies, waits for them, and re-layouts  10.4 us

profile of v1, /device:TPU:0, one launch (start us, length us, event | category | flops | bytes accessed | tf_op | source)
XLA Modules:
  0.0 32.9 jit_solution(1941853895453766417)
XLA Ops:
  0.6 0.0 copy-start.7
  0.6 0.0 copy-start.6
  0.7 0.0 copy-start.12
  0.7 0.0 copy-start.13
  0.7 0.6 %copy-done.7 = s32[1024]{0:T(1024)S(1)} copy-done((s32[1024]{0:T(1024)S(1)}, s32[1024]{0:T(1024)}, u32[]{:S(2)}) %copy-start.7) | copy-done | bytes 4120
  1.3 0.0 copy-done.6
  1.3 0.0 copy-done.12
  1.3 0.0 copy-done.13
  1.3 0.0 copy-start
  1.3 0.9 %copy-done = f32[64,384]{1,0:T(8,128)S(1)} copy-done((f32[64,384]{1,0:T(8,128)S(1)}, f32[64,384]{1,0:T(8,128)}, u32[]{:S(2)}) %copy-start) | copy-done | bytes 98328
  2.2 0.0 copy-start.1
  2.2 0.8 %copy-done.1 = bf16[128,128]{1,0:T(8,128)(2,1)S(1)} copy-done((bf16[128,128]{1,0:T(8,128)(2,1)S(1)}, bf16[128,128]{1,0:T(8,128)(2,1)}, u32[]{:S(2)}) %copy-start.1) | copy-done | bytes 32792
  3.0 0.0 copy-start.2
  3.0 0.8 %copy-done.2 = bf16[128,128]{1,0:T(8,128)(2,1)S(1)} copy-done((bf16[128,128]{1,0:T(8,128)(2,1)S(1)}, bf16[128,128]{1,0:T(8,128)(2,1)}, u32[]{:S(2)}) %copy-start.2) | copy-done | bytes 32792
  3.8 0.0 copy-start.3
  3.8 0.8 %copy-done.3 = f32[64,64]{1,0:T(8,128)S(1)} copy-done((f32[64,64]{1,0:T(8,128)S(1)}, f32[64,64]{1,0:T(8,128)}, u32[]{:S(2)}) %copy-start.3) | copy-done | bytes 16408
  4.5 0.0 copy-start.4
  4.5 0.8 %copy-done.4 = bf16[128,128]{1,0:T(8,128)(2,1)S(1)} copy-done((bf16[128,128]{1,0:T(8,128)(2,1)S(1)}, bf16[128,128]{1,0:T(8,128)(2,1)}, u32[]{:S(2)}) %copy-start.4) | copy-done | bytes 32792
  5.3 0.0 copy-start.5
  5.3 0.7 %copy-done.5 = f32[3,1024]{1,0:T(4,128)S(1)} copy-done((f32[3,1024]{1,0:T(4,128)S(1)}, f32[3,1024]{1,0:T(4,128)}, u32[]{:S(2)}) %copy-start.5) | copy-done | bytes 12312
  6.0 0.0 copy-start.8
  6.0 0.7 %copy-done.8 = s32[1024]{0:T(1024)S(1)} copy-done((s32[1024]{0:T(1024)S(1)}, s32[1024]{0:T(1024)}, u32[]{:S(2)}) %copy-start.8) | copy-done | bytes 4120
  6.7 0.0 copy-start.9
  6.7 0.7 %copy-done.9 = f32[8,64]{1,0:T(8,128)S(1)} copy-done((f32[8,64]{1,0:T(8,128)S(1)}, f32[8,64]{1,0:T(8,128)}, u32[]{:S(2)}) %copy-start.9) | copy-done | bytes 2072
  7.4 0.0 copy-start.10
  7.4 0.7 %copy-done.10 = f32[8,128]{1,0:T(8,128)S(1)} copy-done((f32[8,128]{1,0:T(8,128)S(1)}, f32[8,128]{1,0:T(8,128)}, u32[]{:S(2)}) %copy-start.10) | copy-done | bytes 4120
  8.1 0.0 copy-start.11
  8.1 0.7 %copy-done.11 = f32[3,128]{1,0:T(4,128)S(1)} copy-done((f32[3,128]{1,0:T(4,128)S(1)}, f32[3,128]{1,0:T(4,128)}, u32[]{:S(2)}) %copy-start.11) | copy-done | bytes 1560
  8.7 0.0 copy-start.14
  8.7 0.7 %copy-done.14 = f32[8]{0:T(128)S(1)} copy-done((f32[8]{0:T(128)S(1)}, f32[8]{0:T(128)}, u32[]{:S(2)}) %copy-start.14) | copy-done | bytes 56
  9.4 21.8 %shard_map.166 = (f32[1,128]{1,0:T(1,128)S(1)}, f32[3,128]{1,0:T(4,128)S(1)}, bf16[128,128]{1,0:T(8,128)(2,1)S(1)}) custom-call(bf16[128,128]{1,0:T(8,128)(2,1)S(1)} %copy-done.1, s32[1,128]{1,0:T(1,128)S(1)} %bitcast.9, s32[1,16]{1,0:T(1,128)S(1)} %bitcast.10, s32[1,1024]{1,0:T(1,128)S(1)} %bitcast.6, s32[1,1024]{1,0:T(1,128)S(1)} %bitcast.7, ...), custom_call_target="tpu_custom_call" | custom-call | tf_op jit(solution)/shard_map/pallas_call | solution.py:602
  31.2 0.5 %copy.21 = f32[128]{0:T(128)} copy(f32[128]{0:T(128)S(1)} %bitcast.11) | data formatting | bytes 1024
  31.7 0.6 %copy.22 = f32[3,128]{1,0:T(4,128)} copy(f32[3,128]{1,0:T(4,128)S(1)} %get-tuple-element.13) | data formatting | bytes 3072
  32.3 0.6 %copy.23 = bf16[128,128]{1,0:T(8,128)(2,1)} copy(bf16[128,128]{1,0:T(8,128)(2,1)S(1)} %get-tuple-element.14) | data formatting | bytes 65536
Async XLA Ops:
  0.6 0.7 %copy-start.7 = (s32[1024]{0:T(1024)S(1)}, s32[1024]{0:T(1024)}, u32[]{:S(2)}) copy-start(s32[1024]{0:T(1024)} %param.19) | copy-start | bytes 12292
  0.6 0.7 %copy-start.6 = (s32[1024]{0:T(1024)S(1)}, s32[1024]{0:T(1024)}, u32[]{:S(2)}) copy-start(s32[1024]{0:T(1024)} %param.18) | copy-start | bytes 12292
  0.7 0.7 %copy-start.12 = (s32[128]{0:T(128)S(1)}, s32[128]{0:T(128)}, u32[]{:S(2)}) copy-start(s32[128]{0:T(128)} %param.16) | copy-start | bytes 1540
  0.7 0.7 %copy-start.13 = (s32[16]{0:T(128)S(1)}, s32[16]{0:T(128)}, u32[]{:S(2)}) copy-start(s32[16]{0:T(128)} %param.17) | copy-start | bytes 196
  1.3 0.9 %copy-start = (f32[64,384]{1,0:T(8,128)S(1)}, f32[64,384]{1,0:T(8,128)}, u32[]{:S(2)}) copy-start(f32[64,384]{1,0:T(8,128)} %three_ref.1) | copy-start | bytes 294916
  2.2 0.8 %copy-start.1 = (bf16[128,128]{1,0:T(8,128)(2,1)S(1)}, bf16[128,128]{1,0:T(8,128)(2,1)}, u32[]{:S(2)}) copy-start(bf16[128,128]{1,0:T(8,128)(2,1)} %feats_ref.1) | copy-start | bytes 98308
  3.0 0.8 %copy-start.2 = (bf16[128,128]{1,0:T(8,128)(2,1)S(1)}, bf16[128,128]{1,0:T(8,128)(2,1)}, u32[]{:S(2)}) copy-start(bf16[128,128]{1,0:T(8,128)(2,1)} %w_up_ref.1) | copy-start | bytes 98308
  3.8 0.8 %copy-start.3 = (f32[64,64]{1,0:T(8,128)S(1)}, f32[64,64]{1,0:T(8,128)}, u32[]{:S(2)}) copy-start(f32[64,64]{1,0:T(8,128)} %two_ref.1) | copy-start | bytes 49156
  4.5 0.8 %copy-start.4 = (bf16[128,128]{1,0:T(8,128)(2,1)S(1)}, bf16[128,128]{1,0:T(8,128)(2,1)}, u32[]{:S(2)}) copy-start(bf16[128,128]{1,0:T(8,128)(2,1)} %w_mix_ref.1) | copy-start | bytes 98308
  5.3 0.7 %copy-start.5 = (f32[3,1024]{1,0:T(4,128)S(1)}, f32[3,1024]{1,0:T(4,128)}, u32[]{:S(2)}) copy-start(f32[3,1024]{1,0:T(4,128)} %disp_ref.1) | copy-start | bytes 36868
  6.0 0.7 %copy-start.8 = (s32[1024]{0:T(1024)S(1)}, s32[1024]{0:T(1024)}, u32[]{:S(2)}) copy-start(s32[1024]{0:T(1024)} %param.20) | copy-start | bytes 12292
  6.7 0.7 %copy-start.9 = (f32[8,64]{1,0:T(8,128)S(1)}, f32[8,64]{1,0:T(8,128)}, u32[]{:S(2)}) copy-start(f32[8,64]{1,0:T(8,128)} %one_ref.1) | copy-start | bytes 6148
  7.4 0.7 %copy-start.10 = (f32[8,128]{1,0:T(8,128)S(1)}, f32[8,128]{1,0:T(8,128)}, u32[]{:S(2)}) copy-start(f32[8,128]{1,0:T(8,128)} %read_ref.1) | copy-start | bytes 12292
  8.1 0.7 %copy-start.11 = (f32[3,128]{1,0:T(4,128)S(1)}, f32[3,128]{1,0:T(4,128)}, u32[]{:S(2)}) copy-start(f32[3,128]{1,0:T(4,128)} %power_ref.1) | copy-start | bytes 4612
  8.7 0.7 %copy-start.14 = (f32[8]{0:T(128)S(1)}, f32[8]{0:T(128)}, u32[]{:S(2)}) copy-start(f32[8]{0:T(128)} %base_ref.1) | copy-start | bytes 100

commit v2 on v1

--- a/solution.py
+++ b/solution.py
@@ -139,7 +139,9 @@
             self.members[index].append(g)
             self.sub_of[g] = sub
         self.own = self.index((1, 1, 1))
-        self.others = [d for d in range(self.count) if d != self.own]
+        self.others = sorted(
+            (d for d in range(self.count) if d != self.own), key=lambda d: self.shift(d)[0] == 0
+        )
         self.start, self.rows, self.block_start = {}, {}, {}
         total = 0
         for d in self.others:
@@ -182,20 +184,20 @@
 
 def kernel(
     plan,
-    feats_ref,
-    species_ref,
-    export_ref,
-    first_ref,
-    second_ref,
-    live_ref,
-    disp_ref,
-    w_up_ref,
-    one_ref,
-    two_ref,
-    three_ref,
-    power_ref,
-    w_mix_ref,
-    read_ref,
+    feats_far,
+    species_far,
+    export_far,
+    first_far,
+    second_far,
+    live_far,
+    disp_far,
+    w_up_far,
+    one_far,
+    two_far,
+    three_far,
+    power_far,
+    w_mix_far,
+    read_far,
     base_ref,
     energy_ref,
     force_ref,
@@ -222,6 +224,21 @@
     r1,
     s2,
     r2,
+    load_sem,
+    feats_ref,
+    species_ref,
+    export_ref,
+    first_ref,
+    second_ref,
+    live_ref,
+    disp_ref,
+    w_up_ref,
+    one_ref,
+    two_ref,
+    three_ref,
+    power_ref,
+    w_mix_ref,
+    read_ref,
 ):
     atoms, channels = feats_ref.shape
     pairs = first_ref.shape[1]
@@ -245,6 +262,28 @@
     for d in plan.others:
         pl.semaphore_signal(barrier, inc=1, device_id=device(d, 1), device_id_type=MESH)
 
+    order = (
+        (first_far, first_ref),
+        (second_far, second_ref),
+        (feats_far, feats_ref),
+        (disp_far, disp_ref),
+        (live_far, live_ref),
+        (export_far, export_ref),
+        (one_far, one_ref),
+        (two_far, two_ref),
+        (three_far, three_ref),
+        (w_up_far, w_up_ref),
+        (w_mix_far, w_mix_ref),
+        (species_far, species_ref),
+        (power_far, power_ref),
+        (read_far, read_ref),
+    )
+    loads = [
+        pltpu.make_async_copy(far, near, load_sem.at[i]) for i, (far, near) in enumerate(order)
+    ]
+    for load in loads:
+        load.start()
+
     lane = lax.broadcasted_iota(jnp.int32, (1, width), 1)
     block = jnp.maximum(lane - pad, 0) >> 4
     offsets = plan.lane_offsets(block)
@@ -252,6 +291,8 @@
     lane_sub = plan.sub(offsets)
     ghost_base = plan.index(offsets, turned=True) * slots
 
+    for load in loads[:6]:
+        load.wait()
     first = first_ref[...]
     second = second_ref[...]
     live = live_ref[...].astype(F32)
@@ -317,6 +358,8 @@
         copy.start()
         first_copies.append(copy)
 
+    for load in loads[6:]:
+        load.wait()
     one = split_weights(one_ref[...])
     two = split_weights(two_ref[...])
     three = split_weights(three_ref[...])
@@ -348,10 +391,11 @@
         return inverse, n
 
     def scaled_hot(hot, rows, at):
-        hot = hot.astype(F32)
         lanes = hot.shape[1]
         for k in range(9):
-            s_ref[k * atoms : (k + 1) * atoms, at : at + lanes] = (hot * rows[k]).astype(BF16)
+            scale = jnp.broadcast_to(rows[k], (16, lanes)).astype(BF16)
+            scale = jnp.concatenate([scale] * (atoms // 16), axis=0)
+            s_ref[k * atoms : (k + 1) * atoms, at : at + lanes] = hot * scale
 
     def messages(radial_at, up, at):
         lanes = up.shape[1]
@@ -380,8 +424,41 @@
     info_in[...] = jnp.zeros((width, 128), BF16)
     ghost_in[...] = jnp.zeros((plan.count * slots, channels), BF16)
 
+    row = lax.broadcasted_iota(jnp.int32, (width, 128), 0)
+    row_block = jnp.maximum(row - pad, 0) >> 4
+    row_sub = plan.sub(plan.lane_offsets(row_block))
+    column = lax.broadcasted_iota(jnp.int32, (width, 128), 1) >> 4
+    mask_one = (column == row_sub).astype(F32).astype(BF16)
+    mask_two = (column == row_sub + 1).astype(F32).astype(BF16)
+    pick_row = lax.broadcasted_iota(jnp.int32, (16, 128), 0)
+    pick_at = lax.broadcasted_iota(jnp.int32, (16, 128), 1) & 15
+    pick = jnp.where(pick_at < 9, (pick_at * 11) >> 5, pick_at - 6) == pick_row
+    pick = pick.astype(F32).astype(BF16)
+    power = [tables[:, l : l + 1] for l in range(3)]
+    species = species_ref[...]
+    picker = (lax.broadcasted_iota(jnp.int32, (128, atoms), 0) == species + 3).astype(F32)
+    read_rows = lax.dot_general(
+        tables,
+        picker,
+        (((1,), (0,)), ((), ())),
+        precision=lax.Precision.HIGHEST,
+        preferred_element_type=F32,
+    )
+    base = jnp.zeros((1, atoms), F32)
+    for s in range(read_ref.shape[0]):
+        base = base + jnp.where(species == s, base_ref[s], 0.0)
+
+    def amps_of(degree, start, stop):
+        low, high = DEGREE_ROWS[degree]
+        return nt(
+            m_ref[degree * channels : (degree + 1) * channels, start:stop],
+            s_ref[low * atoms : high * atoms, start:stop],
+        )
+
+    early = [amps_of(l, 0, cut) + amps_of(l, pairs, pairs + cut) for l in range(3)]
+
     for copy in first_copies:
-        copy.wait()
+        copy.wait_recv()
     for d in plan.others:
         at = plan.start[d]
         ghost_in[d * slots : (d + 1) * slots, :] = recv_one[at : at + slots, :]
@@ -392,15 +469,8 @@
             edge_in[here, :] = recv_one[spot : spot + slots, :]
             info_in[here, :] = tile
 
-    row = lax.broadcasted_iota(jnp.int32, (width, 128), 0)
-    row_block = jnp.maximum(row - pad, 0) >> 4
-    row_sub = plan.sub(plan.lane_offsets(row_block))
-    column = lax.broadcasted_iota(jnp.int32, (width, 128), 1) >> 4
-    info_own = jnp.where(column == row_sub, info_in[...].astype(F32), 0.0).astype(BF16)
-    pick_row = lax.broadcasted_iota(jnp.int32, (16, 128), 0)
-    pick_at = lax.broadcasted_iota(jnp.int32, (16, 128), 1) & 15
-    pick = jnp.where(pick_at < 9, (pick_at * 11) >> 5, pick_at - 6) == pick_row
-    incoming = nt(pick.astype(F32).astype(BF16), info_own)
+    info_own = info_in[...] * mask_one
+    incoming = nt(pick, info_own)
     slot_in = incoming[4:5, :].astype(jnp.int32)
     slot_hot = (lax.broadcasted_iota(jnp.int32, (slots, width), 0) == slot_in).astype(F32)
     export_rows = jnp.broadcast_to(export_ref[...].astype(F32), (8, slots))
@@ -411,7 +481,8 @@
     for i, v in enumerate((vx, vy, vz)):
         back.append(-jnp.where(own_lane, v[:, cut:], incoming[i : i + 1, :]))
     hot_b = (lax.broadcasted_iota(jnp.int32, (atoms, width), 0) == target).astype(F32)
-    hot_back[...] = hot_b.astype(BF16)
+    hot_b = hot_b.astype(BF16)
+    hot_back[...] = hot_b
     inverse_b, n_b = geometry(*back, pairs)
     scaled_hot(hot_b, harmonic_rows(n_b, weight_b), pairs + cut)
     ghost_up = nt(w_up_t, ghost_in[...]).astype(BF16)
@@ -420,9 +491,8 @@
 
     amps = []
     for l, (low, high) in enumerate(DEGREE_ROWS):
-        sums = nt(m_ref[l * channels : (l + 1) * channels, :], s_ref[low * atoms : high * atoms, :])
+        sums = early[l] + amps_of(l, cut, pairs) + amps_of(l, pairs + cut, 2 * pairs)
         amps += [sums[:, i * atoms : (i + 1) * atoms] for i in range(high - low)]
-    power = [tables[:, l : l + 1] for l in range(3)]
     product = amps[0]
     for l, (low, high) in enumerate(DEGREE_ROWS):
         total = amps[low] * amps[low]
@@ -430,18 +500,6 @@
             total = total + amps[k] * amps[k]
         product = product + power[l] * total
     mixed = nn(w_mix_t, product.astype(BF16))
-    species = species_ref[...]
-    picker = (lax.broadcasted_iota(jnp.int32, (128, atoms), 0) == species + 3).astype(F32)
-    read_rows = lax.dot_general(
-        tables,
-        picker,
-        (((1,), (0,)), ((), ())),
-        precision=lax.Precision.HIGHEST,
-        preferred_element_type=F32,
-    )
-    base = jnp.zeros((1, atoms), F32)
-    for s in range(read_ref.shape[0]):
-        base = base + jnp.where(species == s, base_ref[s], 0.0)
     sigmoid = jax.nn.sigmoid(mixed)
     energy_ref[...] = jnp.sum(mixed * sigmoid * read_rows, axis=0, keepdims=True) + base
     grad_mixed = (read_rows * sigmoid * (1.0 + mixed * (1.0 - sigmoid))).astype(BF16)
@@ -547,7 +605,7 @@
     info_in[...] = edge_force.astype(BF16)
 
     for copy in second_copies:
-        copy.wait()
+        copy.wait_recv()
     offered_grad, offered_force = 0.0, 0.0
     for d in plan.others:
         at = plan.start[d]
@@ -559,7 +617,7 @@
             here = slice(pad + slots * g, pad + slots * (g + 1))
             edge_in[here, :] = recv_two[spot : spot + slots, :]
             info_in[here, :] = tile
-    info_own = jnp.where(column == row_sub + 1, info_in[...].astype(F32), 0.0).astype(BF16)
+    info_own = info_in[...] * mask_two
     offered_column = lax.broadcasted_iota(jnp.int32, (slots, 128), 1)
     offered_force = jnp.where(offered_column < 16, offered_force, 0.0)
     window_hot = hot_one[:, cut:]
@@ -569,8 +627,19 @@
     total = force[0:3, :] + force[3:6, :]
     for j in range(8):
         total = total + remote_force[16 * j : 16 * j + 3, :] + remote_force[16 * j + 3 : 16 * j + 6, :]
+    for copy in first_copies + second_copies:
+        copy.wait_send()
     force_ref[...] = total
     grad_ref[...] = nt(grad_up.astype(BF16), w_up).astype(BF16)
+
+
+def place(a_ref, b_ref, c_ref, a_out, b_out, c_out, sem):
+    pairs = ((a_ref, a_out), (b_ref, b_out), (c_ref, c_out))
+    copies = [pltpu.make_async_copy(a, b, sem.at[i]) for i, (a, b) in enumerate(pairs)]
+    for copy in copies:
+        copy.start()
+    for copy in copies:
+        copy.wait()
 
 
 def on_device(plan, *args):
@@ -599,6 +668,22 @@
     ghosts = plan.count * slots
     vmem = pl.BlockSpec(memory_space=pltpu.VMEM)
     smem = pl.BlockSpec(memory_space=pltpu.SMEM)
+    operands = (
+        node_feats,
+        species.reshape(1, atoms),
+        export_index.reshape(1, slots),
+        pair_first.reshape(1, pairs),
+        pair_second.reshape(1, pairs),
+        pair_live.reshape(1, pairs),
+        displacement,
+        w_up,
+        radial_one,
+        radial_two,
+        radial_three,
+        power_weight,
+        w_mix,
+        read_table,
+    )
     energy, forces, grad = pl.pallas_call(
         functools.partial(kernel, plan),
         out_shape=(
@@ -606,7 +691,7 @@
             jax.ShapeDtypeStruct((3, atoms), F32),
             jax.ShapeDtypeStruct((atoms, channels), BF16),
         ),
-        in_specs=[vmem] * 14 + [smem],
+        in_specs=[pl.BlockSpec(memory_space=pltpu.HBM)] * 14 + [smem],
         out_specs=(vmem,) * 3,
         scratch_shapes=[pltpu.VMEM((plan.total, channels), BF16)] * 4
         + [
@@ -625,27 +710,22 @@
             pltpu.VMEM((channels, 9 * atoms), BF16),
             pltpu.VMEM((9 * channels, atoms), BF16),
         ]
-        + [pltpu.SemaphoreType.DMA((plan.count,))] * 4,
+        + [pltpu.SemaphoreType.DMA((plan.count,))] * 4
+        + [pltpu.SemaphoreType.DMA((len(operands),))]
+        + [pltpu.VMEM(v.shape, v.dtype) for v in operands],
         compiler_params=pltpu.CompilerParams(
-            collective_id=0, has_side_effects=True, vmem_limit_bytes=48 * 1024 * 1024
+            collective_id=0, has_side_effects=True, vmem_limit_bytes=64 * 1024 * 1024
         ),
-    )(
-        node_feats,
-        species.reshape(1, atoms),
-        export_index.reshape(1, slots),
-        pair_first.reshape(1, pairs),
-        pair_second.reshape(1, pairs),
-        pair_live.reshape(1, pairs),
-        displacement,
-        w_up,
-        radial_one,
-        radial_two,
-        radial_three,
-        power_weight,
-        w_mix,
-        read_table,
-        base_energy,
-    )
+    )(*operands, base_energy)
+    results = (energy, forces, grad)
+    energy, forces, grad = pl.pallas_call(
+        place,
+        out_shape=tuple(jax.ShapeDtypeStruct(v.shape, v.dtype) for v in results),
+        in_specs=[vmem] * 3,
+        out_specs=(pl.BlockSpec(memory_space=pl.ANY),) * 3,
+        scratch_shapes=[pltpu.SemaphoreType.DMA((3,))],
+        compiler_params=pltpu.CompilerParams(has_side_effects=True),
+    )(*results)
     return energy.reshape(atoms), forces, grad
 
 

time: 33.5 us -> 24.1 us (0.72); the launches traced: 32.9 us -> 23.9 us
  local copies, waits for them, and re-layouts: 10.4 us -> 0 us
  Pallas kernels: 21.8 us -> 23.3 us
    unnamed x33 -> x0, local copies, waits for them, and re-layouts: 10.4 us -> none
    pallas_call x0 -> x1, Pallas kernels: none -> 1.42 us  [on_device(): pl.pallas_call(place, out_shape=tuple((jax.ShapeDtypeStruct(v.shape, v.dt...]
where the time goes in v2:
time: 24.1 us; the launch traced here: 23.9 us
  Pallas kernels  23.3 us (97%)
  between operations  0.64 us (3%)
    pallas_call x1, Pallas kernels, on_device(): pl.pallas_call(functools.partial(kernel, plan), out_shape=(jax.ShapeDtype...  21.8 us
    pallas_call x1, Pallas kernels, on_device(): pl.pallas_call(place, out_shape=tuple((jax.ShapeDtypeStruct(v.shape, v.dt...  1.42 us

profile of v2, /device:TPU:0, one launch (start us, length us, event | category | flops | bytes accessed | tf_op | source)
XLA Modules:
  0.0 23.9 jit_solution(13302670061572688449)
XLA Ops:
  0.6 21.8 %shard_map.166 = (f32[1,128]{1,0:T(1,128)}, f32[3,128]{1,0:T(4,128)}, bf16[128,128]{1,0:T(8,128)(2,1)}) custom-call(bf16[128,128]{1,0:T(8,128)(2,1)} %feats_far.1, s32[1,128]{1,0:T(1,128)} %bitcast.9, s32[1,16]{1,0:T(1,128)} %bitcast.10, s32[1,1024]{1,0:T(1,128)} %bitcast.6, s32[1,1024]{1,0:T(1,128)} %bitcast.7, s32[1,1024]{1,0:T(1,128)} %bitcast.8, ...), custom_call_target="tpu_custom_call" | custom-call | tf_op jit(solution)/shard_map/pallas_call | solution.py:687
  22.5 1.4 %shard_map.167 = (f32[1,128]{1,0:T(1,128)}, f32[3,128]{1,0:T(4,128)}, bf16[128,128]{1,0:T(8,128)(2,1)}) custom-call(f32[1,128]{1,0:T(1,128)} %get-tuple-element.9.a_ref, f32[3,128]{1,0:T(4,128)} %get-tuple-element.10.b_ref, bf16[128,128]{1,0:T(8,128)(2,1)} %get-tuple-element.11.c_ref), custom_call_target="tpu_custom_call" | custom-call | tf_op jit(solution)/shard_map/pallas_call | solution.py:721

commit v3 on v2

--- a/solution.py
+++ b/solution.py
@@ -198,7 +198,7 @@
     power_far,
     w_mix_far,
     read_far,
-    base_ref,
+    base_far,
     energy_ref,
     force_ref,
     grad_ref,
@@ -239,6 +239,7 @@
     power_ref,
     w_mix_ref,
     read_ref,
+    base_ref,
 ):
     atoms, channels = feats_ref.shape
     pairs = first_ref.shape[1]
@@ -277,6 +278,7 @@
         (species_far, species_ref),
         (power_far, power_ref),
         (read_far, read_ref),
+        (base_far, base_ref),
     )
     loads = [
         pltpu.make_async_copy(far, near, load_sem.at[i]) for i, (far, near) in enumerate(order)
@@ -667,7 +669,6 @@
     width = pairs - cut
     ghosts = plan.count * slots
     vmem = pl.BlockSpec(memory_space=pltpu.VMEM)
-    smem = pl.BlockSpec(memory_space=pltpu.SMEM)
     operands = (
         node_feats,
         species.reshape(1, atoms),
@@ -683,6 +684,7 @@
         power_weight,
         w_mix,
         read_table,
+        base_energy,
     )
     energy, forces, grad = pl.pallas_call(
         functools.partial(kernel, plan),
@@ -691,7 +693,7 @@
             jax.ShapeDtypeStruct((3, atoms), F32),
             jax.ShapeDtypeStruct((atoms, channels), BF16),
         ),
-        in_specs=[pl.BlockSpec(memory_space=pltpu.HBM)] * 14 + [smem],
+        in_specs=[pl.BlockSpec(memory_space=pltpu.HBM)] * 15,
         out_specs=(vmem,) * 3,
         scratch_shapes=[pltpu.VMEM((plan.total, channels), BF16)] * 4
         + [
@@ -712,11 +714,12 @@
         ]
         + [pltpu.SemaphoreType.DMA((plan.count,))] * 4
         + [pltpu.SemaphoreType.DMA((len(operands),))]
-        + [pltpu.VMEM(v.shape, v.dtype) for v in operands],
+        + [pltpu.VMEM(v.shape, v.dtype) for v in operands[:-1]]
+        + [pltpu.SMEM(base_energy.shape, F32)],
         compiler_params=pltpu.CompilerParams(
             collective_id=0, has_side_effects=True, vmem_limit_bytes=64 * 1024 * 1024
         ),
-    )(*operands, base_energy)
+    )(*operands)
     results = (energy, forces, grad)
     energy, forces, grad = pl.pallas_call(
         place,

time: 24.1 us -> 23.5 us (0.975)
  Pallas kernels: 23.3 us -> 22.6 us
    pallas_call x1, Pallas kernels: 21.8 us -> 21.2 us  [on_device(): pl.pallas_call(functools.partial(kernel, plan), out_shape=(jax.ShapeDtype...]
where the time goes in v3:
time: 23.5 us; the launch traced here: 23.2 us
  Pallas kernels  22.6 us (96%)
  between operations  0.64 us (3%)
    pallas_call x1, Pallas kernels, on_device(): pl.pallas_call(functools.partial(kernel, plan), out_shape=(jax.ShapeDtype...  21.2 us
    pallas_call x1, Pallas kernels, on_device(): pl.pallas_call(place, out_shape=tuple((jax.ShapeDtypeStruct(v.shape, v.dt...  1.42 us

profile of v3, /device:TPU:0, one launch (start us, length us, event | category | flops | bytes accessed | tf_op | source)
XLA Modules:
  0.0 23.2 jit_solution(9000476337849782419)
XLA Ops:
  0.6 21.2 %shard_map.166 = (f32[1,128]{1,0:T(1,128)}, f32[3,128]{1,0:T(4,128)}, bf16[128,128]{1,0:T(8,128)(2,1)}) custom-call(bf16[128,128]{1,0:T(8,128)(2,1)} %feats_far.1, s32[1,128]{1,0:T(1,128)} %bitcast.9, s32[1,16]{1,0:T(1,128)} %bitcast.10, s32[1,1024]{1,0:T(1,128)} %bitcast.6, s32[1,1024]{1,0:T(1,128)} %bitcast.7, s32[1,1024]{1,0:T(1,128)} %bitcast.8, ...), custom_call_target="tpu_custom_call" | custom-call | tf_op jit(solution)/shard_map/pallas_call | solution.py:689
  21.8 1.4 %shard_map.167 = (f32[1,128]{1,0:T(1,128)}, f32[3,128]{1,0:T(4,128)}, bf16[128,128]{1,0:T(8,128)(2,1)}) custom-call(f32[1,128]{1,0:T(1,128)} %get-tuple-element.9.a_ref, f32[3,128]{1,0:T(4,128)} %get-tuple-element.10.b_ref, bf16[128,128]{1,0:T(8,128)(2,1)} %get-tuple-element.11.c_ref), custom_call_target="tpu_custom_call" | custom-call | tf_op jit(solution)/shard_map/pallas_call | solution.py:724
